TPU v7x, 32 devices: a whole 2x2x4 slice. The times are simulated.
32 devices in a mesh: groups: 2 (over y), gx: 8 (over z, x), gy: 2 (over core).
Axes of the slice: x: 2, y: 2, z: 4, core: 2. Of those that a mesh axis runs over, the one named last changes fastest.
Arguments:
- field: bfloat16 [16, 64, 64, 128], P(None, ('groups', 'gx'), 'gy'), parts along dimension 1, may hold values from -6 to 6
- cotangent: bfloat16 [16, 64, 64, 128], P(None, ('groups', 'gx'), 'gy'), parts along dimension 1, may hold values from -6 to 6
- spectral_weight: bfloat16 [2, 16, 16, 16384], P(None, None, None, ('gx', 'gy')), may hold values from -1 to 1
- point_weight: bfloat16 [16, 16], replicated, may hold values from -1.5 to 1.5
- bias: float32 [16], replicated, may hold values from -3 to 3
Outputs:
- layer_out: bfloat16 [16, 64, 64, 128], P(None, ('groups', 'gx'), 'gy'), parts along dimension 1
- field_grad: bfloat16 [16, 64, 64, 128], P(None, ('groups', 'gx'), 'gy'), parts along dimension 1
- weight_grad: float32 [4, 16, 16, 16384], P('groups', None, None, ('gx', 'gy')), parts along dimension 0
There are 2 independent parts, one for each index of `groups`. A program takes and returns all parts, laid end to end along the dimension named above; an argument that names none is the same for every part. Nothing has to cross between parts.
All inputs are finite; a program needn't handle non-finite values.
Results may differ from a plain program's by a relative error of at most 0.0079.
Values may be sent and summed in bfloat16 or wider, within the bound.
A program may use at most 128 MiB of HBM per device.

v0:
```python
import math

import jax
import jax.numpy as jnp
from jax import lax
from jax.sharding import PartitionSpec as P

MX = 32
MY = 32
MZ = 16


def phase_tables(count, length, offset, rows, signed):
    position = offset + jnp.arange(rows, dtype=jnp.int32)
    freq = jnp.arange(count, dtype=jnp.int32)
    if signed:
        freq = jnp.where(freq >= count // 2, freq + (length - count), freq)
    turns = freq[:, None] * position[None, :] % length
    angle = turns.astype(jnp.float32) * (2.0 * math.pi / length)
    return (jnp.cos(angle).astype(jnp.bfloat16), jnp.sin(angle).astype(jnp.bfloat16))


def z_transform(block, cos_z, sin_z):
    chans, rows_x, rows_y, nz_len = block.shape
    kept = cos_z.shape[0]
    tables = jnp.concatenate([cos_z, sin_z], axis=0)
    flat = jnp.dot(block.reshape(-1, nz_len), tables.T, preferred_element_type=jnp.float32)
    flat = flat.reshape(chans, rows_x, rows_y, 2 * kept)
    both = jnp.transpose(flat, (0, 3, 1, 2))
    return (both[:, :kept], both[:, kept:])


def point_mix(matrix, grid):
    chans = grid.shape[0]
    flat = jnp.dot(matrix, grid.reshape(chans, -1), preferred_element_type=jnp.float32)
    return flat.reshape(grid.shape)


def forward_yz(block, y_start, zscale, ny_total):
    hp = lax.Precision.HIGHEST
    rows_y = block.shape[2]
    nz_len = block.shape[3]
    cos_z, sin_z = phase_tables(MZ, nz_len, 0, nz_len, False)
    zscale_b = zscale[None, :, None, None]
    z_cos, z_sin = z_transform(block, cos_z, sin_z)
    part_r = z_cos * zscale_b
    part_i = -z_sin * zscale_b
    cos_y, sin_y = phase_tables(MY, ny_total, y_start, rows_y, True)
    cos_y = cos_y.astype(jnp.float32)
    sin_y = sin_y.astype(jnp.float32)
    out_r = jnp.einsum("ckxy,jy->cjkx", part_r, cos_y, precision=hp) + jnp.einsum(
        "ckxy,jy->cjkx", part_i, sin_y, precision=hp
    )
    out_i = jnp.einsum("ckxy,jy->cjkx", part_i, cos_y, precision=hp) - jnp.einsum(
        "ckxy,jy->cjkx", part_r, sin_y, precision=hp
    )
    return (out_r, out_i)


def forward_x(part_r, part_i, x_start, nx_total):
    hp = lax.Precision.HIGHEST
    chans = part_r.shape[0]
    rows_x = part_r.shape[3]
    cos_x, sin_x = phase_tables(MX, nx_total, x_start, rows_x, True)
    cos_x = cos_x.astype(jnp.float32)
    sin_x = sin_x.astype(jnp.float32)
    out_r = jnp.einsum("cjkx,ix->cjki", part_r, cos_x, precision=hp) + jnp.einsum(
        "cjkx,ix->cjki", part_i, sin_x, precision=hp
    )
    out_i = jnp.einsum("cjkx,ix->cjki", part_i, cos_x, precision=hp) - jnp.einsum(
        "cjkx,ix->cjki", part_r, sin_x, precision=hp
    )
    return jnp.stack([out_r.reshape(chans, -1), out_i.reshape(chans, -1)])


def inverse_modes(modes, x_start, y_start, zweight, nx_total, ny_total, rows_x, rows_y, nz_len):
    hp = lax.Precision.HIGHEST
    chans = modes.shape[1]
    values = modes.astype(jnp.float32).reshape(2, chans, MY, MZ, MX)
    mode_r = values[0]
    mode_i = values[1]
    cos_x, sin_x = phase_tables(MX, nx_total, x_start, rows_x, True)
    cos_x = cos_x.astype(jnp.float32)
    sin_x = sin_x.astype(jnp.float32)
    step_r = jnp.einsum("cjki,ix->cxjk", mode_r, cos_x, precision=hp) - jnp.einsum(
        "cjki,ix->cxjk", mode_i, sin_x, precision=hp
    )
    step_i = jnp.einsum("cjki,ix->cxjk", mode_i, cos_x, precision=hp) + jnp.einsum(
        "cjki,ix->cxjk", mode_r, sin_x, precision=hp
    )
    cos_y, sin_y = phase_tables(MY, ny_total, y_start, rows_y, True)
    cos_y = cos_y.astype(jnp.float32)
    sin_y = sin_y.astype(jnp.float32)
    next_r = jnp.einsum("cxjk,jy->cxyk", step_r, cos_y, precision=hp) - jnp.einsum(
        "cxjk,jy->cxyk", step_i, sin_y, precision=hp
    )
    next_i = jnp.einsum("cxjk,jy->cxyk", step_i, cos_y, precision=hp) + jnp.einsum(
        "cxjk,jy->cxyk", step_r, sin_y, precision=hp
    )
    cos_z, sin_z = phase_tables(MZ, nz_len, 0, nz_len, False)
    cos_z = cos_z.astype(jnp.float32)
    sin_z = sin_z.astype(jnp.float32)
    next_r = next_r * zweight
    next_i = next_i * zweight
    return jnp.einsum("cxyk,kz->cxyz", next_r, cos_z, precision=hp) - jnp.einsum(
        "cxyk,kz->cxyz", next_i, sin_z, precision=hp
    )


def channel_mix(spectrum, weight):
    hp = lax.Precision.HIGHEST
    w_r = weight[0].astype(jnp.float32)
    w_i = weight[1].astype(jnp.float32)
    out_r = jnp.einsum("im,iom->om", spectrum[0], w_r, precision=hp) - jnp.einsum(
        "im,iom->om", spectrum[1], w_i, precision=hp
    )
    out_i = jnp.einsum("im,iom->om", spectrum[1], w_r, precision=hp) + jnp.einsum(
        "im,iom->om", spectrum[0], w_i, precision=hp
    )
    return jnp.stack([out_r, out_i])


def mix_grads(spectrum, mixed_grad, weight):
    hp = lax.Precision.HIGHEST
    w_r = weight[0].astype(jnp.float32)
    w_i = weight[1].astype(jnp.float32)
    grad_r = jnp.einsum("om,im->iom", mixed_grad[0], spectrum[0], precision=hp) + jnp.einsum(
        "om,im->iom", mixed_grad[1], spectrum[1], precision=hp
    )
    grad_i = jnp.einsum("om,im->iom", mixed_grad[1], spectrum[0], precision=hp) - jnp.einsum(
        "om,im->iom", mixed_grad[0], spectrum[1], precision=hp
    )
    back_r = jnp.einsum("iom,om->im", w_r, mixed_grad[0], precision=hp) + jnp.einsum(
        "iom,om->im", w_i, mixed_grad[1], precision=hp
    )
    back_i = jnp.einsum("iom,om->im", w_r, mixed_grad[1], precision=hp) - jnp.einsum(
        "iom,om->im", w_i, mixed_grad[0], precision=hp
    )
    return (jnp.stack([grad_r, grad_i]), jnp.stack([back_r, back_i]))


def owned_spectrum(block, x_start, y_start, zscale, nx_total, ny_total):
    part_r, part_i = forward_yz(block, y_start, zscale, ny_total)
    whole = forward_x(part_r, part_i, x_start, nx_total)
    return lax.psum_scatter(whole, ("gx", "gy"), scatter_dimension=2, tiled=True)


def all_modes(owned_block):
    return lax.all_gather(owned_block, ("gx", "gy"), axis=2, tiled=True)


def on_device(field, cotangent, spectral_weight, point_weight, bias):
    rows_x = field.shape[1]
    rows_y = field.shape[2]
    nz_len = field.shape[3]
    nx_total = rows_x * lax.axis_size("gx")
    ny_total = rows_y * lax.axis_size("gy")
    total_cells = nx_total * ny_total * nz_len
    mode_count = MX * MY * MZ
    x_start = lax.axis_index("gx") * rows_x
    y_start = lax.axis_index("gy") * rows_y
    zindex = jnp.arange(MZ, dtype=jnp.int32)
    forward_scale = jnp.full((MZ,), 1.0 / math.sqrt(total_cells), jnp.float32)
    inverse_scale = jnp.where(zindex == 0, 1.0, 2.0).astype(jnp.float32) / math.sqrt(
        2.0 * mode_count
    )
    spectrum = owned_spectrum(field, x_start, y_start, forward_scale, nx_total, ny_total)
    mixed = channel_mix(spectrum, spectral_weight).astype(jnp.bfloat16)
    mixed_all = all_modes(mixed)
    spectral_out = inverse_modes(
        mixed_all, x_start, y_start, inverse_scale, nx_total, ny_total, rows_x, rows_y, nz_len
    )
    pre = spectral_out + point_mix(point_weight.T, field) + bias[:, None, None, None]
    layer_out = jax.nn.gelu(pre).astype(jnp.bfloat16)
    pre_grad = jax.vjp(jax.nn.gelu, pre)[1](cotangent.astype(jnp.float32))[0].astype(jnp.bfloat16)
    mixed_grad = owned_spectrum(pre_grad, x_start, y_start, inverse_scale, nx_total, ny_total)
    weight_grad, spectrum_grad = mix_grads(spectrum, mixed_grad, spectral_weight)
    weight_grad = weight_grad * math.sqrt(2.0 * mode_count / total_cells)
    grad_all = all_modes(spectrum_grad.astype(jnp.bfloat16))
    local = point_mix(point_weight, pre_grad)
    spectral = inverse_modes(
        grad_all, x_start, y_start, forward_scale, nx_total, ny_total, rows_x, rows_y, nz_len
    )
    field_grad = (local + spectral).astype(jnp.bfloat16)
    return (layer_out, field_grad, weight_grad)


def solution(mesh):
    in_specs = (
        P(None, ("groups", "gx"), "gy", None),
        P(None, ("groups", "gx"), "gy", None),
        P(None, None, None, ("gx", "gy")),
        P(),
        P(),
    )
    out_specs = (
        P(None, ("groups", "gx"), "gy", None),
        P(None, ("groups", "gx"), "gy", None),
        P("groups", None, None, ("gx", "gy")),
    )
    return jax.shard_map(
        on_device, mesh=mesh, in_specs=in_specs, out_specs=out_specs, check_vma=False
    )
```

profile of v0, /device:TPU:0, one launch (start us, length us, event | category | flops | bytes accessed | tf_op | source)
XLA Modules:
  0.0 357.1 jit_solution(3522790761459180196)
XLA Ops:
  7.3 1.3 convolution_bitcast_fusion
  12.0 3.5 fusion.104
  15.5 5.2 %fusion.100 = f32[16,32,16,32]{3,1,2,0:T(8,128)} fusion(f32[16,32,16,4]{1,2,3,0:T(8,128)S(1)} %fusion.54, s32[4]{0:T(128)S(1)} %iota_add_fusion), kind=kOutput, calls=%fused_computation.125 | convolution fusion | flops 12584832 | bytes 1179664 | tf_op jit(solution)/shard_map/cjkx,ix->cjki/dot_general | solution.py:70
  20.7 3.5 convolution_add_fusion.1
  24.2 5.2 %copy.22 = f32[16,32,16,32]{3,2,1,0:T(8,128)} copy(f32[16,32,16,32]{3,1,2,0:T(8,128)S(1)} %convolution_add_fusion.1) | data formatting | bytes 2097152 | tf_op jit(solution)/shard_map/add | solution.py:67
  29.4 3.5 stack_reshape.12
  32.9 5.6 %convolution_subtract_fusion.1 = f32[16,32,16,32]{3,1,2,0:T(8,128)S(1)} fusion(f32[16,32,16,32]{3,1,2,0:T(8,128)} %fusion.100, f32[16,32,16,4]{1,2,3,0:T(8,128)S(1)} %fusion.55, s32[4]{0:T(128)S(1)} %iota_add_fusion), kind=kOutput, calls=%fused_computation.3 | convolution fusion | flops 12846976 | bytes 2228240 | tf_op jit(solution)/shard_map/cjkx,ix->cjki/dot_general | solution.py:70
  38.5 5.2 %copy.25 = f32[16,32,16,32]{3,2,1,0:T(8,128)} copy(f32[16,32,16,32]{3,1,2,0:T(8,128)S(1)} %convolution_subtract_fusion.1) | data formatting | bytes 2097152 | tf_op jit(solution)/shard_map/sub | solution.py:70
  43.7 3.5 stack_reshape.13
  47.2 1.5 pad_maximum_fusion
  48.8 64.3 %reduce-scatter.3.cloned.1.call-done = f32[2,16,1024]{2,1,0:T(8,128)} async-done(((f32[2,16,16384]{2,1,0:T(8,128)}), f32[2,16,1024]{2,1,0:T(8,128)}) %reduce-scatter.3.cloned.1.call-update) | async-done | bytes 131088 | tf_op jit(solution)/shard_map/reduce_scatter | solution.py:145
  113.1 0.9 slice_bitcast_fusion.3
  115.6 1.4 fusion.78
  117.0 36.1 %all-gather.3.cloned.1.call-done = bf16[2,16,16384]{2,1,0:T(8,128)(2,1)} async-done(((bf16[2,16,1024]{2,1,0:T(8,128)(2,1)}), bf16[2,16,16384]{2,1,0:T(8,128)(2,1)}) %all-gather.3.cloned.1.call-update) | async-done | bytes 1048592 | tf_op jit(solution)/shard_map/all_gather | solution.py:149
  153.1 2.2 fusion.268
  155.3 2.5 squeeze.57
  157.8 3.7 %fusion.8 = f32[4,16,32,16]{2,0,3,1:T(4,128)} fusion(bf16[16,32,16,32]{3,2,1,0:T(8,128)(2,1)S(1)} %squeeze.57, s32[4]{0:T(128)S(1)} %iota_add_fusion), kind=kOutput, calls=%fused_computation.16 | convolution fusion | flops 2099072 | bytes 655376 | tf_op jit(solution)/shard_map/cjki,ix->cxjk/dot_general | solution.py:88
  161.5 3.7 %fusion.10 = f32[4,16,32,16]{2,0,3,1:T(4,128)} fusion(bf16[16,32,16,32]{3,2,1,0:T(8,128)(2,1)S(1)} %squeeze.57, s32[4]{0:T(128)S(1)} %iota_add_fusion), kind=kOutput, calls=%fused_computation.18 | convolution fusion | flops 2099072 | bytes 655376 | tf_op jit(solution)/shard_map/cjki,ix->cxjk/dot_general | solution.py:85
  165.2 2.9 squeeze.56
  168.1 4.0 %fusion.29 = f32[16,4,32,16]{2,1,3,0:T(4,128)S(1)} fusion(f32[4,16,32,16]{2,0,3,1:T(4,128)} %fusion.8, bf16[16,32,16,32]{3,2,1,0:T(8,128)(2,1)S(1)} %squeeze.56, s32[4]{0:T(128)S(1)} %iota_add_fusion), kind=kOutput, calls=%fused_computation.47 | convolution fusion | flops 2131840 | bytes 786448 | tf_op jit(solution)/shard_map/cjki,ix->cxjk/dot_general | solution.py:88
  172.6 2.9 fusion.23
  177.1 1.0 fusion.156
  178.2 3.0 fusion.58
  181.2 0.9 convolution_bitcast_fusion.2
  183.7 3.6 %fusion.98 = f32[16,32,16,32]{3,1,2,0:T(8,128)S(1)} fusion(f32[16,32,16,4]{1,2,3,0:T(8,128)S(1)} %fusion.49, s32[4]{0:T(128)S(1)} %iota_add_fusion), kind=kOutput, calls=%fused_computation.123 | convolution fusion | flops 12584832 | bytes 1179664 | tf_op jit(solution)/shard_map/cjkx,ix->cjki/dot_general | solution.py:67
  187.9 5.0 %fusion.94 = f32[16,32,16,32]{3,1,2,0:T(8,128)} fusion(f32[16,32,16,4]{1,2,3,0:T(8,128)S(1)} %fusion.48, s32[4]{0:T(128)S(1)} %iota_add_fusion), kind=kOutput, calls=%fused_computation.119 | convolution fusion | flops 12584832 | bytes 1179664 | tf_op jit(solution)/shard_map/cjkx,ix->cjki/dot_general | solution.py:70
  192.9 3.5 convolution_add_fusion
  196.5 5.2 %copy.35 = f32[16,32,16,32]{3,2,1,0:T(8,128)} copy(f32[16,32,16,32]{3,1,2,0:T(8,128)S(1)} %convolution_add_fusion) | data formatting | bytes 2097152 | tf_op jit(solution)/shard_map/add | solution.py:67
  201.7 3.5 stack_reshape.14
  205.2 5.6 %convolution_subtract_fusion = f32[16,32,16,32]{3,1,2,0:T(8,128)S(1)} fusion(f32[16,32,16,32]{3,1,2,0:T(8,128)} %fusion.94, f32[16,32,16,4]{1,2,3,0:T(8,128)S(1)} %fusion.49, s32[4]{0:T(128)S(1)} %iota_add_fusion), kind=kOutput, calls=%fused_computation.1 | convolution fusion | flops 12846976 | bytes 2228240 | tf_op jit(solution)/shard_map/cjkx,ix->cjki/dot_general | solution.py:70
  210.8 5.2 %copy.38 = f32[16,32,16,32]{3,2,1,0:T(8,128)} copy(f32[16,32,16,32]{3,1,2,0:T(8,128)S(1)} %convolution_subtract_fusion) | data formatting | bytes 2097152 | tf_op jit(solution)/shard_map/sub | solution.py:70
  216.0 4.3 %stack_reshape.15 = f32[1,16,16384]{2,1,0:T(8,128)} reshape(f32[16,32,16,32]{3,2,1,0:T(8,128)} %copy.38) | data formatting | bytes 2097152 | tf_op jit(solution)/shard_map/stack;reshape | solution.py:73
  220.3 2.8 pad_maximum_fusion.1
  223.2 60.6 %reduce-scatter.5.cloned.1.call-done = f32[2,16,1024]{2,1,0:T(8,128)} async-done(((f32[2,16,16384]{2,1,0:T(8,128)}), f32[2,16,1024]{2,1,0:T(8,128)}) %reduce-scatter.5.cloned.1.call-update) | async-done | bytes 131088 | tf_op jit(solution)/shard_map/reduce_scatter | solution.py:145
  283.8 0.9 slice_bitcast_fusion.1
  284.7 0.9 fusion.67
  285.6 0.6 pad_maximum_fusion.3
  287.2 1.5 maximum_multiply_fusion
  288.7 34.7 %all-gather.5.cloned.1.call-done = bf16[2,16,16384]{2,1,0:T(8,128)(2,1)} async-done(((bf16[2,16,1024]{2,1,0:T(8,128)(2,1)}), bf16[2,16,16384]{2,1,0:T(8,128)(2,1)}) %all-gather.5.cloned.1.call-update) | async-done | bytes 1048592 | tf_op jit(solution)/shard_map/all_gather | solution.py:149
  323.4 2.3 fusion.267
  325.7 2.7 squeeze.61
  328.4 3.7 %fusion = f32[4,16,32,16]{2,0,3,1:T(4,128)} fusion(bf16[16,32,16,32]{3,2,1,0:T(8,128)(2,1)S(1)} %squeeze.61, s32[4]{0:T(128)S(1)} %iota_add_fusion), kind=kOutput, calls=%fused_computation.8 | convolution fusion | flops 2099072 | bytes 655376 | tf_op jit(solution)/shard_map/cjki,ix->cxjk/dot_general | solution.py:88
  332.1 3.7 %fusion.2 = f32[4,16,32,16]{2,0,3,1:T(4,128)} fusion(bf16[16,32,16,32]{3,2,1,0:T(8,128)(2,1)S(1)} %squeeze.61, s32[4]{0:T(128)S(1)} %iota_add_fusion), kind=kOutput, calls=%fused_computation.10 | convolution fusion | flops 2099072 | bytes 655376 | tf_op jit(solution)/shard_map/cjki,ix->cxjk/dot_general | solution.py:85
  335.7 2.5 squeeze.60
  338.3 4.0 %fusion.41 = f32[16,4,32,16]{2,1,3,0:T(4,128)S(1)} fusion(f32[4,16,32,16]{2,0,3,1:T(4,128)} %fusion, bf16[16,32,16,32]{3,2,1,0:T(8,128)(2,1)S(1)} %squeeze.60, s32[4]{0:T(128)S(1)} %iota_add_fusion), kind=kOutput, calls=%fused_computation.51 | convolution fusion | flops 2131840 | bytes 786448 | tf_op jit(solution)/shard_map/cjki,ix->cxjk/dot_general | solution.py:88
  342.8 2.9 fusion.35
  347.3 1.0 fusion.154
  348.3 1.8 fusion.19
  (57 shorter events, 12.4 us)
Async XLA Ops:
  7.2 108.4 %copy-start = (bf16[16,16]{1,0:T(8,128)(2,1)S(1)}, bf16[16,16]{1,0:T(8,128)(2,1)}, u32[]{:S(2)}) copy-start(bf16[16,16]{1,0:T(8,128)(2,1)} %param.8) | copy-start | bytes 1540
  7.2 105.9 %reduce-scatter.3.cloned.1.call-start = ((), (), s32[]{:S(2)}) async-start(), calls=%async_computation.2 | async-start | bytes 2228224 | tf_op jit(solution)/shard_map/reduce_scatter | solution.py:145
  48.7 65.3 %copy-start.1 = (bf16[2,16,16,1024]{3,2,1,0:T(8,128)(2,1)S(1)}, bf16[2,16,16,1024]{3,2,1,0:T(8,128)(2,1)}, u32[]{:S(2)}) copy-start(bf16[2,16,16,1024]{3,2,1,0:T(8,128)(2,1)} %param.7) | copy-start | bytes 3145732
  48.7 66.4 %copy-start.2 = (bf16[16,4,32,128]{3,2,1,0:T(8,128)(2,1)S(1)}, bf16[16,4,32,128]{3,2,1,0:T(8,128)(2,1)}, u32[]{:S(2)}) copy-start(bf16[16,4,32,128]{3,2,1,0:T(8,128)(2,1)} %param.5) | copy-start | bytes 1572868
  48.7 104.4 %all-gather.3.cloned.1.call-start = ((), (), s32[]{:S(2)}) async-start(), calls=%async_computation.3 | async-start | bytes 1114112 | tf_op jit(solution)/shard_map/all_gather | solution.py:149
  115.0 168.7 %reduce-scatter.5.cloned.1.call-start = ((), (), s32[]{:S(2)}) async-start(), calls=%async_computation.4 | async-start | bytes 2228224 | tf_op jit(solution)/shard_map/reduce_scatter | solution.py:145
  168.1 4.5 %copy-start.4 = (f32[4,16,32,16]{2,0,3,1:T(4,128)S(1)}, f32[4,16,32,16]{2,0,3,1:T(4,128)}, u32[]{:S(2)}) copy-start(f32[4,16,32,16]{2,0,3,1:T(4,128)} %fusion.10) | copy-start | bytes 393220
  176.0 2.1 copy-start.5
  176.0 2.1 copy-start.6
  176.1 2.1 copy-start.7
  223.2 100.2 %all-gather.5.cloned.1.call-start = ((), (), s32[]{:S(2)}) async-start(), calls=%async_computation.5 | async-start | bytes 1114112 | tf_op jit(solution)/shard_map/all_gather | solution.py:149
  338.2 4.5 %copy-start.3 = (f32[4,16,32,16]{2,0,3,1:T(4,128)S(1)}, f32[4,16,32,16]{2,0,3,1:T(4,128)}, u32[]{:S(2)}) copy-start(f32[4,16,32,16]{2,0,3,1:T(4,128)} %fusion.2) | copy-start | bytes 393220
Sparse Core Ops, SparseCore 0:
  48.8 64.2 reduce-scatter.2
  116.1 36.9 all-gather.2
  223.3 60.4 reduce-scatter.4
  286.4 36.9 all-gather.4
where the time goes:
time: 363 us; the launch traced here: 357 us
  waiting for transfers between devices  196 us (54%)
  matrix products  83.4 us (23%)
  local copies, waits for them, and re-layouts  54.4 us (15%)
  between operations  14.7 us (4%)
  other arithmetic  8.71 us (2%)
    reduce_scatter x2, waiting for transfers between devices, owned_spectrum(): lax.psum_scatter(whole, ('gx', 'gy'), scatter_dimension=2, tiled=True)  125 us
    all_gather x2, waiting for transfers between devices, all_modes(): return lax.all_gather(owned_block, ('gx', 'gy'), axis=2, tiled=True)  70.8 us
    another operation x4, local copies, waits for them, and re-layouts, forward_x(): return jnp.stack([out_r.reshape(chans, -1), out_i.reshape(chans, -1)])  14.8 us
    dot_general x2, matrix products, forward_x(): jnp.einsum('cjkx,ix->cjki', part_r, sin_x, precision=hp)  11.2 us
    add x2, local copies, waits for them, and re-layouts, forward_x(): jnp.einsum('cjkx,ix->cjki', part_r, cos_x, precision=hp)  10.4 us
    sub x2, local copies, waits for them, and re-layouts, forward_x(): jnp.einsum('cjkx,ix->cjki', part_i, cos_x, precision=hp)  10.4 us
    dot_general x2, matrix products, forward_x(): jnp.einsum('cjkx,ix->cjki', part_i, cos_x, precision=hp)  10.3 us
    dot_general x2, matrix products, inverse_modes(): jnp.einsum('cjki,ix->cxjk', mode_r, sin_x, precision=hp)  7.94 us
  transfers between devices with their start and end apart: 4, of which 4 were waited for; matrix products, arithmetic and copies ran while one was open for 1% of the time, Pallas kernels for 0%

commit v1 on v0

--- a/solution.py
+++ b/solution.py
@@ -2,7 +2,10 @@
 
 import jax
 import jax.numpy as jnp
+import numpy as np
 from jax import lax
+from jax.experimental import pallas as pl
+from jax.experimental.pallas import tpu as pltpu
 from jax.sharding import PartitionSpec as P
 
 MX = 32
@@ -185,7 +188,343 @@
     return (layer_out, field_grad, weight_grad)
 
 
+BF = jnp.bfloat16
+F32 = jnp.float32
+MESH = pl.DeviceIdType.MESH
+GC = 8
+
+
+def host_tables(count, length, cells, signed):
+    freq = np.arange(count)
+    if signed:
+        freq = np.where(freq >= count // 2, freq + (length - count), freq)
+    turns = (freq[:, None] * cells[None, :]) % length
+    angle = turns.astype(np.float32) * np.float32(2.0 * math.pi / length)
+    rounded = [np.asarray(fn(angle)).astype(BF).astype(np.float32) for fn in (np.cos, np.sin)]
+    return rounded[0], rounded[1]
+
+
+def constant_tables(gx, gy, rows_x, rows_y, nz_len):
+    nx_total, ny_total = rows_x * gx, rows_y * gy
+    cos_x, sin_x = host_tables(MX, nx_total, np.arange(nx_total), True)
+    cos_y, sin_y = host_tables(MY, ny_total, np.arange(ny_total), True)
+    cos_z, sin_z = host_tables(MZ, nz_len, np.arange(nz_len), False)
+    eye_c, eye_x, eye_k = np.eye(GC), np.eye(rows_x), np.eye(MZ)
+    cy = cos_y.reshape(MY, gy, rows_y)
+    sy = sin_y.reshape(MY, gy, rows_y)
+    y_fwd = np.stack([np.einsum("jgy,cd->gjcdy", t, eye_c) for t in (cy, sy)], axis=1)
+    y_fwd = y_fwd.reshape(gy, 2 * MY * GC, GC * rows_y)
+    y_inv = np.stack([np.einsum("jgy,cd->gcyjd", t, eye_c) for t in (cy, -sy)], axis=3)
+    y_inv = y_inv.reshape(gy, GC * rows_y, 2 * MY * GC)
+    z_pairs = np.stack([np.stack([cos_z, -sin_z]), np.stack([-sin_z, -cos_z])])
+    z_fwd = np.einsum("arkz,xw->axzrkw", z_pairs, eye_x)
+    z_fwd = z_fwd.reshape(2 * rows_x * nz_len, 2 * MZ * rows_x)
+    i_pairs = np.stack([np.stack([cos_z, -sin_z]), np.stack([sin_z, cos_z])])
+    z_inv = np.einsum("arkz,xw->rkwaxz", i_pairs, eye_x)
+    z_inv = z_inv.reshape(2 * MZ * rows_x, 2 * rows_x * nz_len)
+    x_pairs = np.stack([np.stack([cos_x, -sin_x]), np.stack([sin_x, cos_x])])
+    x_pairs = x_pairs.reshape(2, 2, MX, gx, rows_x)
+    x_fwd = np.einsum("rsigx,kl->grkxsli", x_pairs, eye_k)
+    x_fwd = x_fwd.reshape(gx * 2 * MZ * rows_x, 2 * MZ * MX)
+    x_inv = np.ascontiguousarray(x_fwd.T)
+    return [t.astype(BF) for t in (y_fwd, y_inv, z_fwd, z_inv, x_fwd, x_inv)]
+
+
+def dot(a, b):
+    return jnp.dot(a, b, preferred_element_type=F32)
+
+
+def split_dot(a, b):
+    high = a.astype(BF)
+    low = (a - high.astype(F32)).astype(BF)
+    both = dot(jnp.concatenate([high, low], axis=0), b)
+    return both[: a.shape[0]] + both[a.shape[0] :]
+
+
+def fused(
+    gx, gy, zscales, inv_wg,
+    field, cot, weight, point, bias, y_fwd, y_inv, z_fwd, z_inv, x_fwd, x_inv,
+    layer_out, field_grad, weight_grad,
+    send_a, send_b, recv, grid_f, grid_g, local, spec, grad, mode_grad, mix_a, mix_b, send_sem, recv_sem,
+):
+    peers = gx * gy
+    chans, rows_x, rows_y, nz_len = field.shape
+    half_rows = GC * rows_y
+    halves = chans // GC
+    slab = recv.shape[2]
+    slab_half = slab // halves
+    lanes = recv.shape[3]
+    me_x, me_y = lax.axis_index("gx"), lax.axis_index("gy")
+    me = me_x * gy + me_y
+    half_modes = MZ * MX
+
+    def peer(step):
+        other = lax.rem(me + step, peers)
+        return other, {"gx": other // gy, "gy": lax.rem(other, gy)}
+
+    barrier = pltpu.get_barrier_semaphore()
+
+    def greet(step, carry):
+        pl.semaphore_signal(barrier, inc=1, device_id=peer(step)[1], device_id_type=MESH)
+        return carry
+
+    lax.fori_loop(1, peers, greet, 0)
+
+    def copy_to(phase, buffer, step):
+        other, where = peer(step)
+        source = buffer.at[other] if buffer.shape[0] == peers else buffer.at[other // gy]
+        return pltpu.make_async_remote_copy(
+            src_ref=source,
+            dst_ref=recv.at[phase, me],
+            send_sem=send_sem.at[phase, other],
+            recv_sem=recv_sem.at[phase, me],
+            device_id=where,
+            device_id_type=MESH,
+        )
+
+    def send(phase, buffer):
+        def one(step, carry):
+            copy_to(phase, buffer, step).start()
+            return carry
+
+        lax.fori_loop(1, peers, one, 0)
+        own = buffer[me] if buffer.shape[0] == peers else buffer[me_x]
+        recv[phase, me] = own
+
+    def receive(phase, buffer):
+        def one(step, carry):
+            other, where = peer(step)
+            pltpu.make_async_remote_copy(
+                src_ref=recv.at[phase, other],
+                dst_ref=recv.at[phase, other],
+                send_sem=send_sem.at[phase, other],
+                recv_sem=recv_sem.at[phase, other],
+                device_id=where,
+                device_id_type=MESH,
+            ).wait_recv()
+            return carry
+
+        lax.fori_loop(1, peers, one, 0)
+
+    def drain(phase, buffer):
+        def one(step, carry):
+            copy_to(phase, buffer, step).wait_send()
+            return carry
+
+        lax.fori_loop(1, peers, one, 0)
+
+    def zweight(width, scale_zero, scale_rest):
+        lane = lax.broadcasted_iota(jnp.int32, (1, width), 1)
+        k = lax.rem(lane // rows_x, MZ)
+        return jnp.where(k == 0, scale_zero, scale_rest).astype(F32)
+
+    fwd_scale, inv_zero, inv_rest = zscales
+
+    def to_modes(grid, buffer, scale):
+        for h in range(halves):
+            table = y_fwd[me_y]
+            after_y = dot(table, grid[h * half_rows : (h + 1) * half_rows, :])
+            rows = after_y.shape[0] // 2
+            both = jnp.concatenate([after_y[:rows], after_y[rows:]], axis=1).astype(BF)
+            out = (dot(both, z_fwd[...]) * scale).astype(BF)
+            buffer[:, h * slab_half : (h + 1) * slab_half, :] = out.reshape(peers, slab_half, lanes)
+
+    def owned(phase):
+        parts = []
+        for s in range(gx):
+            total = recv[phase, s * gy].astype(F32)
+            for t in range(1, gy):
+                total = total + recv[phase, s * gy + t].astype(F32)
+            parts.append(total)
+        return split_dot(jnp.concatenate(parts, axis=1), x_fwd[...])
+
+    def store_owned(values, store):
+        for h in range(halves):
+            for j in range(slab_half // GC):
+                rows = values[h * slab_half + j * GC : h * slab_half + (j + 1) * GC]
+                for r in range(2):
+                    store[r, h * GC : (h + 1) * GC, j * half_modes : (j + 1) * half_modes] = rows[
+                        :, r * half_modes : (r + 1) * half_modes
+                    ]
+
+    def to_slabs(store, buffer, scale):
+        rows = []
+        for h in range(halves):
+            for j in range(slab_half // GC):
+                rows.append(
+                    jnp.concatenate(
+                        [
+                            store[r, h * GC : (h + 1) * GC, j * half_modes : (j + 1) * half_modes]
+                            for r in range(2)
+                        ],
+                        axis=1,
+                    )
+                )
+        values = jnp.concatenate(rows, axis=0).astype(BF)
+        out = (dot(values, x_inv[...]) * scale).astype(BF)
+        for s in range(gx):
+            buffer[s] = out[:, s * lanes : (s + 1) * lanes]
+
+    def to_grid(phase, h):
+        modes = recv[phase, :, h * slab_half : (h + 1) * slab_half, :]
+        modes = modes.reshape(peers * slab_half, lanes)
+        after_z = dot(modes, z_inv[...]).astype(BF)
+        width = rows_x * nz_len
+        both = jnp.concatenate([after_z[:, :width], after_z[:, width:]], axis=0)
+        return dot(y_inv[me_y], both)
+
+    def spread(matrix):
+        n = chans * rows_y
+        row = lax.broadcasted_iota(jnp.int32, (n, chans), 0) // rows_y
+        pick = (row == lax.broadcasted_iota(jnp.int32, (n, chans), 1)).astype(BF)
+        col = lax.broadcasted_iota(jnp.int32, (chans, n), 1) // rows_y
+        pick_t = (col == lax.broadcasted_iota(jnp.int32, (chans, n), 0)).astype(BF)
+        wide = dot(dot(pick, matrix).astype(BF), pick_t)
+        diag = lax.rem(lax.broadcasted_iota(jnp.int32, (n, n), 0), rows_y) == lax.rem(
+            lax.broadcasted_iota(jnp.int32, (n, n), 1), rows_y
+        )
+        return jnp.where(diag, wide, 0.0).astype(BF)
+
+    for c in range(chans):
+        for x in range(rows_x):
+            grid_f[c * rows_y : (c + 1) * rows_y, x * nz_len : (x + 1) * nz_len] = field[c, x]
+    to_modes(grid_f, send_a.at[0], fwd_scale)
+    pl.semaphore_wait(barrier, peers - 1)
+    send(0, send_a.at[0])
+    mix_a[...] = spread(point[...].T)
+    mix_b[...] = spread(point[...])
+    local[...] = dot(mix_a[...], grid_f[...])
+    receive(0, send_a.at[0])
+
+    store_owned(owned(0), spec)
+    half = half_modes
+    for j in range(slab_half // GC):
+        span = slice(j * half, (j + 1) * half)
+        mixed_r = jnp.zeros((chans, half), F32)
+        mixed_i = jnp.zeros((chans, half), F32)
+        for c in range(chans):
+            w_r = weight[0, c, :, span].astype(F32)
+            w_i = weight[1, c, :, span].astype(F32)
+            s_r = spec[0, c : c + 1, span]
+            s_i = spec[1, c : c + 1, span]
+            mixed_r = mixed_r + (s_r * w_r - s_i * w_i)
+            mixed_i = mixed_i + (s_i * w_r + s_r * w_i)
+        grad[0, :, span] = mixed_r
+        grad[1, :, span] = mixed_i
+    to_slabs(grad, send_b.at[0], zweight(gx * lanes, inv_zero, inv_rest))
+    send(1, send_b.at[0])
+    receive(1, send_b.at[0])
+
+    a = math.sqrt(2.0 / math.pi)
+    for h in range(halves):
+        rows = slice(h * half_rows, (h + 1) * half_rows)
+        pre_half = to_grid(1, h) + local[rows, :]
+        for c in range(GC):
+            o = h * GC + c
+            pre = pre_half[c * rows_y : (c + 1) * rows_y] + bias[o]
+            square = pre * pre
+            t = jnp.tanh(a * pre * (1.0 + 0.044715 * square))
+            cdf = 0.5 * (1.0 + t)
+            out = (pre * cdf).astype(BF)
+            slope = cdf + 0.5 * pre * (1.0 - t * t) * (a * (1.0 + 3.0 * 0.044715 * square))
+            for x in range(rows_x):
+                cols = slice(x * nz_len, (x + 1) * nz_len)
+                layer_out[o, x] = out[:, cols]
+                grid_g[o * rows_y : (o + 1) * rows_y, cols] = (
+                    cot[o, x].astype(F32) * slope[:, cols]
+                ).astype(BF)
+    to_modes(grid_g, send_a.at[1], zweight(lanes, inv_zero, inv_rest))
+    send(2, send_a.at[1])
+    local[...] = dot(mix_b[...], grid_g[...])
+    receive(2, send_a.at[1])
+
+    store_owned(owned(2), grad)
+    for j in range(slab_half // GC):
+        span = slice(j * half, (j + 1) * half)
+        g_r = grad[0, :, span]
+        g_i = grad[1, :, span]
+        for c in range(chans):
+            w_r = weight[0, c, :, span].astype(F32)
+            w_i = weight[1, c, :, span].astype(F32)
+            mode_grad[0, c : c + 1, span] = jnp.sum(w_r * g_r + w_i * g_i, axis=0, keepdims=True)
+            mode_grad[1, c : c + 1, span] = jnp.sum(w_r * g_i - w_i * g_r, axis=0, keepdims=True)
+    to_slabs(mode_grad, send_b.at[1], fwd_scale)
+    send(3, send_b.at[1])
+    for j in range(slab_half // GC):
+        span = slice(j * half, (j + 1) * half)
+        g_r = grad[0, :, span] * inv_wg
+        g_i = grad[1, :, span] * inv_wg
+        for c in range(chans):
+            s_r = spec[0, c : c + 1, span]
+            s_i = spec[1, c : c + 1, span]
+            weight_grad[0, c, :, span] = g_r * s_r + g_i * s_i
+            weight_grad[1, c, :, span] = g_i * s_r - g_r * s_i
+    receive(3, send_b.at[1])
+    for h in range(halves):
+        total = to_grid(3, h) + local[h * half_rows : (h + 1) * half_rows, :]
+        out = total.astype(BF)
+        for c in range(GC):
+            for x in range(rows_x):
+                field_grad[h * GC + c, x] = out[
+                    c * rows_y : (c + 1) * rows_y, x * nz_len : (x + 1) * nz_len
+                ]
+    drain(0, send_a.at[0])
+    drain(1, send_b.at[0])
+    drain(2, send_a.at[1])
+    drain(3, send_b.at[1])
+
+
+def on_device_fused(gx, gy, field, cotangent, spectral_weight, point_weight, bias):
+    chans, rows_x, rows_y, nz_len = field.shape
+    peers = gx * gy
+    owned_modes = spectral_weight.shape[3]
+    total_cells = gx * gy * rows_x * rows_y * nz_len
+    mode_count = MX * MY * MZ
+    inv = 1.0 / math.sqrt(2.0 * mode_count)
+    zscales = (1.0 / math.sqrt(total_cells), inv, 2.0 * inv)
+    wg_scale = math.sqrt(2.0 * mode_count / total_cells)
+    tables = [jnp.asarray(t) for t in constant_tables(gx, gy, rows_x, rows_y, nz_len)]
+    slab = MY // peers * chans
+    lanes = 2 * MZ * rows_x
+    rows, width = chans * rows_y, rows_x * nz_len
+    vmem = pl.BlockSpec(memory_space=pltpu.VMEM)
+    smem = pl.BlockSpec(memory_space=pltpu.SMEM)
+
+    def body(*refs):
+        fused(gx, gy, zscales, wg_scale, *refs)
+
+    return pl.pallas_call(
+        body,
+        out_shape=(
+            jax.ShapeDtypeStruct(field.shape, BF),
+            jax.ShapeDtypeStruct(field.shape, BF),
+            jax.ShapeDtypeStruct(spectral_weight.shape, F32),
+        ),
+        in_specs=[vmem, vmem, vmem, vmem, smem] + [vmem] * 6,
+        out_specs=(vmem, vmem, vmem),
+        scratch_shapes=[
+            pltpu.VMEM((2, peers, slab, lanes), BF),
+            pltpu.VMEM((2, gx, slab, lanes), BF),
+            pltpu.VMEM((4, peers, slab, lanes), BF),
+            pltpu.VMEM((rows, width), BF),
+            pltpu.VMEM((rows, width), BF),
+            pltpu.VMEM((rows, width), F32),
+            pltpu.VMEM((2, chans, owned_modes), F32),
+            pltpu.VMEM((2, chans, owned_modes), F32),
+            pltpu.VMEM((2, chans, owned_modes), F32),
+            pltpu.VMEM((rows, rows), BF),
+            pltpu.VMEM((rows, rows), BF),
+            pltpu.SemaphoreType.DMA((4, peers)),
+            pltpu.SemaphoreType.DMA((4, peers)),
+        ],
+        compiler_params=pltpu.CompilerParams(
+            collective_id=0, has_side_effects=True, vmem_limit_bytes=48 * 1024 * 1024
+        ),
+    )(field, cotangent, spectral_weight, point_weight, bias, *tables)
+
+
 def solution(mesh):
+    gx, gy = mesh.shape["gx"], mesh.shape["gy"]
     in_specs = (
         P(None, ("groups", "gx"), "gy", None),
         P(None, ("groups", "gx"), "gy", None),
@@ -198,6 +537,15 @@
         P(None, ("groups", "gx"), "gy", None),
         P("groups", None, None, ("gx", "gy")),
     )
+
+    def local_program(field, cotangent, spectral_weight, point_weight, bias):
+        rows_x = field.shape[1]
+        fits = MY % (gx * gy) == 0 and MY // (gx * gy) * GC % 16 == 0
+        fits = fits and 2 * MZ * rows_x == 128 and field.shape[0] % GC == 0
+        if fits:
+            return on_device_fused(gx, gy, field, cotangent, spectral_weight, point_weight, bias)
+        return on_device(field, cotangent, spectral_weight, point_weight, bias)
+
     return jax.shard_map(
-        on_device, mesh=mesh, in_specs=in_specs, out_specs=out_specs, check_vma=False
-    )
+        local_program, mesh=mesh, in_specs=in_specs, out_specs=out_specs, check_vma=False
+    )

time: 363 us -> 49.3 us (0.14); the launches traced: 357 us -> 48.8 us
  waiting for transfers between devices: 196 us -> 0 us
  matrix products: 83.4 us -> 0 us
  local copies, waits for them, and re-layouts: 54.4 us -> 11.7 us
  Pallas kernels: 0 us -> 36.4 us
  between operations: 14.7 us -> 0.67 us
  other arithmetic: 8.71 us -> 0 us
    reduce_scatter x2 -> x0, waiting for transfers between devices: 125 us -> none  [owned_spectrum(): lax.psum_scatter(whole, ('gx', 'gy'), scatter_dimension=2, tiled=True)]
    dot_general x40 -> x0, matrix products: 83.4 us -> none  [the longest x2 11.2 us: forward_x(): jnp.einsum('cjkx,ix->cjki', part_r, sin_x, precision=hp)]
    all_gather x2 -> x0, waiting for transfers between devices: 70.8 us -> none  [all_modes(): return lax.all_gather(owned_block, ('gx', 'gy'), axis=2, tiled=True)]
    pallas_call x0 -> x1, Pallas kernels: none -> 36.4 us  [on_device_fused(): pl.pallas_call(body, out_shape=(jax.ShapeDtypeStruct(field.shape, BF), ja...]
    another operation x4 -> x0, local copies, waits for them, and re-layouts: 14.8 us -> none  [forward_x(): return jnp.stack([out_r.reshape(chans, -1), out_i.reshape(chans, -1)])]
    squeeze x4 -> x0, local copies, waits for them, and re-layouts: 10.6 us -> none  [the longest x2 5.39 us: inverse_modes(): mode_r = values[0]]
    add x2 -> x0, local copies, waits for them, and re-layouts: 10.4 us -> none  [forward_x(): jnp.einsum('cjkx,ix->cjki', part_r, cos_x, precision=hp)]
    sub x2 -> x0, local copies, waits for them, and re-layouts: 10.4 us -> none  [forward_x(): jnp.einsum('cjkx,ix->cjki', part_i, cos_x, precision=hp)]
  transfers between devices with their start and end apart: 4 -> 0, of which waited for: 4 -> 0; matrix products, arithmetic and copies ran while one was open for 1% -> 0% of each run, Pallas kernels for 0% -> 0%
where the time goes in v1:
time: 49.3 us; the launch traced here: 48.8 us
  Pallas kernels  36.4 us (74%)
  local copies, waits for them, and re-layouts  11.7 us (24%)
  between operations  0.67 us (1%)
    pallas_call x1, Pallas kernels, on_device_fused(): pl.pallas_call(body, out_shape=(jax.ShapeDtypeStruct(field.shape, BF), ja...  36.4 us
    unnamed x23, local copies, waits for them, and re-layouts  11.7 us

profile of v1, /device:TPU:0, one launch (start us, length us, event | category | flops | bytes accessed | tf_op | source)
XLA Modules:
  0.0 48.8 jit_solution(17869086013023899646)
XLA Ops:
  0.6 0.0 copy-start
  0.6 1.2 %copy-done = bf16[2,16,16,1024]{3,2,1,0:T(8,128)(2,1)S(1)} copy-done((bf16[2,16,16,1024]{3,2,1,0:T(8,128)(2,1)S(1)}, bf16[2,16,16,1024]{3,2,1,0:T(8,128)(2,1)}, u32[]{:S(2)}) %copy-start) | copy-done | bytes 1048600
  1.9 0.0 copy-start.1
  1.9 1.0 %copy-done.1 = bf16[16,4,32,128]{3,2,1,0:T(8,128)(2,1)S(1)} copy-done((bf16[16,4,32,128]{3,2,1,0:T(8,128)(2,1)S(1)}, bf16[16,4,32,128]{3,2,1,0:T(8,128)(2,1)}, u32[]{:S(2)}) %copy-start.1) | copy-done | bytes 524312
  2.9 0.0 copy-start.2
  2.9 1.0 %copy-done.2 = bf16[16,4,32,128]{3,2,1,0:T(8,128)(2,1)S(1)} copy-done((bf16[16,4,32,128]{3,2,1,0:T(8,128)(2,1)S(1)}, bf16[16,4,32,128]{3,2,1,0:T(8,128)(2,1)}, u32[]{:S(2)}) %copy-start.2) | copy-done | bytes 524312
  3.9 0.0 copy-start.3
  3.9 1.0 %copy-done.3 = bf16[2,256,512]{2,1,0:T(8,128)(2,1)S(1)} copy-done((bf16[2,256,512]{2,1,0:T(8,128)(2,1)S(1)}, bf16[2,256,512]{2,1,0:T(8,128)(2,1)}, u32[]{:S(2)}) %copy-start.3) | copy-done | bytes 524312
  5.0 0.0 copy-start.4
  5.0 1.0 %copy-done.4 = bf16[2,512,256]{2,1,0:T(8,128)(2,1)S(1)} copy-done((bf16[2,512,256]{2,1,0:T(8,128)(2,1)S(1)}, bf16[2,512,256]{2,1,0:T(8,128)(2,1)}, u32[]{:S(2)}) %copy-start.4) | copy-done | bytes 524312
  6.0 0.0 copy-start.5
  6.0 0.9 %copy-done.5 = bf16[128,1024]{1,0:T(8,128)(2,1)S(1)} copy-done((bf16[128,1024]{1,0:T(8,128)(2,1)S(1)}, bf16[128,1024]{1,0:T(8,128)(2,1)}, u32[]{:S(2)}) %copy-start.5) | copy-done | bytes 262168
  7.0 0.0 copy-start.6
  7.0 0.9 %copy-done.6 = bf16[1024,128]{1,0:T(8,128)(2,1)S(1)} copy-done((bf16[1024,128]{1,0:T(8,128)(2,1)S(1)}, bf16[1024,128]{1,0:T(8,128)(2,1)}, u32[]{:S(2)}) %copy-start.6) | copy-done | bytes 262168
  7.9 0.0 copy-start.7
  7.9 0.7 %copy-done.7 = bf16[16,16]{1,0:T(8,128)(2,1)S(1)} copy-done((bf16[16,16]{1,0:T(8,128)(2,1)S(1)}, bf16[16,16]{1,0:T(8,128)(2,1)}, u32[]{:S(2)}) %copy-start.7) | copy-done | bytes 536
  8.6 0.0 copy-start.8
  8.6 0.7 %copy-done.8 = f32[16]{0:T(128)S(1)} copy-done((f32[16]{0:T(128)S(1)}, f32[16]{0:T(128)}, u32[]{:S(2)}) %copy-start.8) | copy-done | bytes 88
  9.3 36.4 %shard_map.130 = (bf16[16,4,32,128]{3,2,1,0:T(8,128)(2,1)S(1)}, bf16[16,4,32,128]{3,2,1,0:T(8,128)(2,1)S(1)}, f32[2,16,16,1024]{3,2,1,0:T(8,128)}) custom-call(bf16[16,4,32,128]{3,2,1,0:T(8,128)(2,1)S(1)} %copy-done.1, bf16[16,4,32,128]{3,2,1,0:T(8,128)(2,1)S(1)} %copy-done.2, bf16[2,16,16,1024]{3,2,1,0:T(8,128)(2,1)S(1)} %copy-done, ...), custom_call_target="tpu_custom_call" | custom-call | tf_op jit(solution)/shard_map/pallas_call | solution.py:496
  45.7 0.0 copy-start.9
  45.7 0.8 %copy.17 = bf16[16,4,32,128]{3,2,1,0:T(8,128)(2,1)} copy(bf16[16,4,32,128]{3,2,1,0:T(8,128)(2,1)S(1)} %get-tuple-element.6) | data formatting | bytes 1048576
  46.5 0.8 %copy.18 = bf16[16,4,32,128]{3,2,1,0:T(8,128)(2,1)} copy(bf16[16,4,32,128]{3,2,1,0:T(8,128)(2,1)S(1)} %get-tuple-element.7) | data formatting | bytes 1048576
  47.3 0.2 copy-done.9
  47.5 1.3 %copy.19 = f32[2,16,16,1024]{3,2,1,0:T(8,128)} copy(f32[2,16,16,1024]{3,2,1,0:T(8,128)S(1)} %copy-done.9) | data formatting | bytes 4194304
Async XLA Ops:
  0.6 1.2 %copy-start = (bf16[2,16,16,1024]{3,2,1,0:T(8,128)(2,1)S(1)}, bf16[2,16,16,1024]{3,2,1,0:T(8,128)(2,1)}, u32[]{:S(2)}) copy-start(bf16[2,16,16,1024]{3,2,1,0:T(8,128)(2,1)} %refs_2_.1) | copy-start | bytes 3145732
  1.9 1.0 %copy-start.1 = (bf16[16,4,32,128]{3,2,1,0:T(8,128)(2,1)S(1)}, bf16[16,4,32,128]{3,2,1,0:T(8,128)(2,1)}, u32[]{:S(2)}) copy-start(bf16[16,4,32,128]{3,2,1,0:T(8,128)(2,1)} %refs_0_.1) | copy-start | bytes 1572868
  2.9 1.0 %copy-start.2 = (bf16[16,4,32,128]{3,2,1,0:T(8,128)(2,1)S(1)}, bf16[16,4,32,128]{3,2,1,0:T(8,128)(2,1)}, u32[]{:S(2)}) copy-start(bf16[16,4,32,128]{3,2,1,0:T(8,128)(2,1)} %refs_1_.1) | copy-start | bytes 1572868
  3.9 1.0 %copy-start.3 = (bf16[2,256,512]{2,1,0:T(8,128)(2,1)S(1)}, bf16[2,256,512]{2,1,0:T(8,128)(2,1)}, u32[]{:S(2)}) copy-start(bf16[2,256,512]{2,1,0:T(8,128)(2,1)} %constant.13.clone.refs_6_) | copy-start | bytes 1572868
  5.0 1.0 %copy-start.4 = (bf16[2,512,256]{2,1,0:T(8,128)(2,1)S(1)}, bf16[2,512,256]{2,1,0:T(8,128)(2,1)}, u32[]{:S(2)}) copy-start(bf16[2,512,256]{2,1,0:T(8,128)(2,1)} %constant.12.clone.refs_5_) | copy-start | bytes 1572868
  6.0 0.9 %copy-start.5 = (bf16[128,1024]{1,0:T(8,128)(2,1)S(1)}, bf16[128,1024]{1,0:T(8,128)(2,1)}, u32[]{:S(2)}) copy-start(bf16[128,1024]{1,0:T(8,128)(2,1)} %constant.15.clone.refs_8_) | copy-start | bytes 786436
  7.0 0.9 %copy-start.6 = (bf16[1024,128]{1,0:T(8,128)(2,1)S(1)}, bf16[1024,128]{1,0:T(8,128)(2,1)}, u32[]{:S(2)}) copy-start(bf16[1024,128]{1,0:T(8,128)(2,1)} %constant.14.clone.refs_7_) | copy-start | bytes 786436
  7.9 0.7 %copy-start.7 = (bf16[16,16]{1,0:T(8,128)(2,1)S(1)}, bf16[16,16]{1,0:T(8,128)(2,1)}, u32[]{:S(2)}) copy-start(bf16[16,16]{1,0:T(8,128)(2,1)} %refs_3_.1) | copy-start | bytes 1540
  8.6 0.7 %copy-start.8 = (f32[16]{0:T(128)S(1)}, f32[16]{0:T(128)}, u32[]{:S(2)}) copy-start(f32[16]{0:T(128)} %refs_4_.1) | copy-start | bytes 196
  45.7 1.8 %copy-start.9 = (f32[2,16,16,1024]{3,2,1,0:T(8,128)S(1)}, f32[2,16,16,1024]{3,2,1,0:T(8,128)}, u32[]{:S(2)}) copy-start(f32[2,16,16,1024]{3,2,1,0:T(8,128)} %get-tuple-element.8) | copy-start | bytes 6291460

commit v2 on v1

--- a/solution.py
+++ b/solution.py
@@ -243,12 +243,14 @@
 
 def fused(
     gx, gy, zscales, inv_wg,
-    field, cot, weight, point, bias, y_fwd, y_inv, z_fwd, z_inv, x_fwd, x_inv,
-    layer_out, field_grad, weight_grad,
-    send_a, send_b, recv, grid_f, grid_g, local, spec, grad, mode_grad, mix_a, mix_b, send_sem, recv_sem,
+    field_h, cot_h, weight_h, point, bias, y_fwd_h, y_inv_h, z_fwd_h, z_inv_h, x_fwd_h, x_inv_h,
+    layer_out_h, field_grad_h, weight_grad_h,
+    field, cot, weight, y_fwd, y_inv, z_fwd, z_inv, x_fwd, x_inv, layer_out, field_grad, weight_grad,
+    send_a, send_b, recv, grid_g, local, spec, grad, mode_grad, mix_a, mix_b, send_sem, recv_sem,
+    load_sem, store_sem,
 ):
     peers = gx * gy
-    chans, rows_x, rows_y, nz_len = field.shape
+    chans, rows_x, rows_y, nz_len = field_h.shape
     half_rows = GC * rows_y
     halves = chans // GC
     slab = recv.shape[2]
@@ -263,6 +265,35 @@
         return other, {"gx": other // gy, "gy": lax.rem(other, gy)}
 
     barrier = pltpu.get_barrier_semaphore()
+    loads = {}
+
+    def load(name, *pairs):
+        copies = []
+        for source, target in pairs:
+            count = sum(len(c) for c in loads.values()) + len(copies)
+            copies.append(pltpu.make_async_copy(source, target, load_sem.at[count]))
+            copies[-1].start()
+        loads[name] = copies
+
+    def loaded(*names):
+        for name in names:
+            for copy in loads[name]:
+                copy.wait()
+
+    def by_x(flat, grid):
+        return [
+            (flat.at[:, x], grid.at[:, :, x * nz_len : (x + 1) * nz_len]) for x in range(rows_x)
+        ]
+
+    load("field", *by_x(field_h, field))
+    load("y_fwd", (y_fwd_h.at[me_y], y_fwd))
+    load("z_fwd", (z_fwd_h, z_fwd))
+    load("x_fwd", (x_fwd_h, x_fwd))
+    load("weight", (weight_h, weight))
+    load("x_inv", (x_inv_h, x_inv))
+    load("z_inv", (z_inv_h, z_inv))
+    load("y_inv", (y_inv_h.at[me_y], y_inv))
+    load("cot", *by_x(cot_h, cot))
 
     def greet(step, carry):
         pl.semaphore_signal(barrier, inc=1, device_id=peer(step)[1], device_id_type=MESH)
@@ -320,10 +351,17 @@
 
     fwd_scale, inv_zero, inv_rest = zscales
 
+    width = rows_x * nz_len
+
+    def grid_half(grid, h):
+        return grid[h * GC : (h + 1) * GC].reshape(half_rows, width)
+
+    def whole(grid):
+        return grid[...].reshape(chans * rows_y, width)
+
     def to_modes(grid, buffer, scale):
         for h in range(halves):
-            table = y_fwd[me_y]
-            after_y = dot(table, grid[h * half_rows : (h + 1) * half_rows, :])
+            after_y = dot(y_fwd[...], grid_half(grid, h))
             rows = after_y.shape[0] // 2
             both = jnp.concatenate([after_y[:rows], after_y[rows:]], axis=1).astype(BF)
             out = (dot(both, z_fwd[...]) * scale).astype(BF)
@@ -369,9 +407,8 @@
         modes = recv[phase, :, h * slab_half : (h + 1) * slab_half, :]
         modes = modes.reshape(peers * slab_half, lanes)
         after_z = dot(modes, z_inv[...]).astype(BF)
-        width = rows_x * nz_len
         both = jnp.concatenate([after_z[:, :width], after_z[:, width:]], axis=0)
-        return dot(y_inv[me_y], both)
+        return dot(y_inv[...], both)
 
     def spread(matrix):
         n = chans * rows_y
@@ -385,18 +422,18 @@
         )
         return jnp.where(diag, wide, 0.0).astype(BF)
 
-    for c in range(chans):
-        for x in range(rows_x):
-            grid_f[c * rows_y : (c + 1) * rows_y, x * nz_len : (x + 1) * nz_len] = field[c, x]
-    to_modes(grid_f, send_a.at[0], fwd_scale)
+    loaded("field", "y_fwd", "z_fwd")
+    to_modes(field, send_a.at[0], fwd_scale)
     pl.semaphore_wait(barrier, peers - 1)
     send(0, send_a.at[0])
     mix_a[...] = spread(point[...].T)
     mix_b[...] = spread(point[...])
-    local[...] = dot(mix_a[...], grid_f[...])
+    local[...] = dot(mix_a[...], whole(field))
     receive(0, send_a.at[0])
 
+    loaded("x_fwd")
     store_owned(owned(0), spec)
+    loaded("weight", "x_inv")
     half = half_modes
     for j in range(slab_half // GC):
         span = slice(j * half, (j + 1) * half)
@@ -415,6 +452,7 @@
     send(1, send_b.at[0])
     receive(1, send_b.at[0])
 
+    loaded("z_inv", "y_inv", "cot")
     a = math.sqrt(2.0 / math.pi)
     for h in range(halves):
         rows = slice(h * half_rows, (h + 1) * half_rows)
@@ -427,15 +465,17 @@
             cdf = 0.5 * (1.0 + t)
             out = (pre * cdf).astype(BF)
             slope = cdf + 0.5 * pre * (1.0 - t * t) * (a * (1.0 + 3.0 * 0.044715 * square))
-            for x in range(rows_x):
-                cols = slice(x * nz_len, (x + 1) * nz_len)
-                layer_out[o, x] = out[:, cols]
-                grid_g[o * rows_y : (o + 1) * rows_y, cols] = (
-                    cot[o, x].astype(F32) * slope[:, cols]
-                ).astype(BF)
+            layer_out[o] = out
+            grid_g[o] = (cot[o].astype(F32) * slope).astype(BF)
+    stores = [
+        pltpu.make_async_copy(s, d, store_sem.at[n])
+        for n, (d, s) in enumerate(by_x(layer_out_h, layer_out))
+    ]
+    for copy in stores:
+        copy.start()
     to_modes(grid_g, send_a.at[1], zweight(lanes, inv_zero, inv_rest))
     send(2, send_a.at[1])
-    local[...] = dot(mix_b[...], grid_g[...])
+    local[...] = dot(mix_b[...], whole(grid_g))
     receive(2, send_a.at[1])
 
     store_owned(owned(2), grad)
@@ -459,19 +499,21 @@
             s_i = spec[1, c : c + 1, span]
             weight_grad[0, c, :, span] = g_r * s_r + g_i * s_i
             weight_grad[1, c, :, span] = g_i * s_r - g_r * s_i
+    stores.append(pltpu.make_async_copy(weight_grad, weight_grad_h, store_sem.at[len(stores)]))
+    stores[-1].start()
     receive(3, send_b.at[1])
     for h in range(halves):
         total = to_grid(3, h) + local[h * half_rows : (h + 1) * half_rows, :]
-        out = total.astype(BF)
-        for c in range(GC):
-            for x in range(rows_x):
-                field_grad[h * GC + c, x] = out[
-                    c * rows_y : (c + 1) * rows_y, x * nz_len : (x + 1) * nz_len
-                ]
+        field_grad[h * GC : (h + 1) * GC] = total.astype(BF).reshape(GC, rows_y, width)
+    for d, s in by_x(field_grad_h, field_grad):
+        stores.append(pltpu.make_async_copy(s, d, store_sem.at[len(stores)]))
+        stores[-1].start()
     drain(0, send_a.at[0])
     drain(1, send_b.at[0])
     drain(2, send_a.at[1])
     drain(3, send_b.at[1])
+    for copy in stores:
+        copy.wait()
 
 
 def on_device_fused(gx, gy, field, cotangent, spectral_weight, point_weight, bias):
@@ -488,7 +530,11 @@
     lanes = 2 * MZ * rows_x
     rows, width = chans * rows_y, rows_x * nz_len
     vmem = pl.BlockSpec(memory_space=pltpu.VMEM)
+    hbm = pl.BlockSpec(memory_space=pltpu.HBM)
     smem = pl.BlockSpec(memory_space=pltpu.SMEM)
+
+    grid = pltpu.VMEM((chans, rows_y, width), BF)
+    held = [t.shape[1:] if n < 2 else t.shape for n, t in enumerate(tables)]
 
     def body(*refs):
         fused(gx, gy, zscales, wg_scale, *refs)
@@ -500,14 +546,20 @@
             jax.ShapeDtypeStruct(field.shape, BF),
             jax.ShapeDtypeStruct(spectral_weight.shape, F32),
         ),
-        in_specs=[vmem, vmem, vmem, vmem, smem] + [vmem] * 6,
-        out_specs=(vmem, vmem, vmem),
+        in_specs=[hbm, hbm, hbm, vmem, smem] + [hbm] * 6,
+        out_specs=(hbm, hbm, hbm),
         scratch_shapes=[
+            grid,
+            grid,
+            pltpu.VMEM(spectral_weight.shape, BF),
+            *[pltpu.VMEM(s, BF) for s in held],
+            grid,
+            grid,
+            pltpu.VMEM(spectral_weight.shape, F32),
             pltpu.VMEM((2, peers, slab, lanes), BF),
             pltpu.VMEM((2, gx, slab, lanes), BF),
             pltpu.VMEM((4, peers, slab, lanes), BF),
-            pltpu.VMEM((rows, width), BF),
-            pltpu.VMEM((rows, width), BF),
+            grid,
             pltpu.VMEM((rows, width), F32),
             pltpu.VMEM((2, chans, owned_modes), F32),
             pltpu.VMEM((2, chans, owned_modes), F32),
@@ -516,9 +568,11 @@
             pltpu.VMEM((rows, rows), BF),
             pltpu.SemaphoreType.DMA((4, peers)),
             pltpu.SemaphoreType.DMA((4, peers)),
+            pltpu.SemaphoreType.DMA((2 * rows_x + 7,)),
+            pltpu.SemaphoreType.DMA((2 * rows_x + 1,)),
         ],
         compiler_params=pltpu.CompilerParams(
-            collective_id=0, has_side_effects=True, vmem_limit_bytes=48 * 1024 * 1024
+            collective_id=0, has_side_effects=True, vmem_limit_bytes=56 * 1024 * 1024
         ),
     )(field, cotangent, spectral_weight, point_weight, bias, *tables)
 

time: 49.3 us -> 40.3 us (0.82)
  local copies, waits for them, and re-layouts: 11.7 us -> 5.23 us
  Pallas kernels: 36.4 us -> 34.2 us
    unnamed x23 -> x5, local copies, waits for them, and re-layouts: 11.7 us -> 5.23 us
    pallas_call x1, Pallas kernels: 36.4 us -> 34.2 us  [on_device_fused(): pl.pallas_call(body, out_shape=(jax.ShapeDtypeStruct(field.shape, BF), ja...]
where the time goes in v2:
time: 40.3 us; the launch traced here: 40.1 us
  Pallas kernels  34.2 us (85%)
  local copies, waits for them, and re-layouts  5.23 us (13%)
  between operations  0.65 us (2%)
    pallas_call x1, Pallas kernels, on_device_fused(): pl.pallas_call(body, out_shape=(jax.ShapeDtypeStruct(field.shape, BF), ja...  34.2 us
    unnamed x5, local copies, waits for them, and re-layouts  5.23 us

profile of v2, /device:TPU:0, one launch (start us, length us, event | category | flops | bytes accessed | tf_op | source)
XLA Modules:
  0.0 40.1 jit_solution(14925219271695948060)
XLA Ops:
  0.6 34.2 %shard_map.130 = (bf16[16,4,32,128]{3,2,1,0:T(8,128)(2,1)}, bf16[16,4,32,128]{3,2,1,0:T(8,128)(2,1)}, f32[2,16,16,1024]{3,2,1,0:T(8,128)}) custom-call(bf16[16,4,32,128]{3,2,1,0:T(8,128)(2,1)} %refs_0_.1, bf16[16,4,32,128]{3,2,1,0:T(8,128)(2,1)} %refs_1_.1, bf16[2,16,16,1024]{3,2,1,0:T(8,128)(2,1)} %refs_2_.1, bf16[16,16]{1,0:T(8,128)(2,1)} %refs_3_.1, ...), custom_call_target="tpu_custom_call" | custom-call | tf_op jit(solution)/shard_map/pallas_call | solution.py:542
  34.8 0.0 copy-start
  34.8 2.0 %copy.17 = bf16[16,4,32,128]{3,2,1,0:T(8,128)(2,1)} copy(bf16[16,4,32,128]{3,2,1,0:T(8,128)(2,1)} %get-tuple-element.6) | data formatting | bytes 1048576
  36.9 1.9 %copy.18 = bf16[16,4,32,128]{3,2,1,0:T(8,128)(2,1)} copy(bf16[16,4,32,128]{3,2,1,0:T(8,128)(2,1)} %get-tuple-element.7) | data formatting | bytes 1048576
  38.7 0.0 copy-done
  38.7 1.3 %copy.19 = f32[2,16,16,1024]{3,2,1,0:T(8,128)} copy(f32[2,16,16,1024]{3,2,1,0:T(8,128)S(1)} %copy-done) | data formatting | bytes 4194304
Async XLA Ops:
  34.8 3.9 %copy-start = (f32[2,16,16,1024]{3,2,1,0:T(8,128)S(1)}, f32[2,16,16,1024]{3,2,1,0:T(8,128)}, u32[]{:S(2)}) copy-start(f32[2,16,16,1024]{3,2,1,0:T(8,128)} %get-tuple-element.8) | copy-start | bytes 6291460

commit v3 on v2

--- a/solution.py
+++ b/solution.py
@@ -1,3 +1,4 @@
+import functools
 import math
 
 import jax
@@ -242,10 +243,10 @@
 
 
 def fused(
-    gx, gy, zscales, inv_wg,
-    field_h, cot_h, weight_h, point, bias, y_fwd_h, y_inv_h, z_fwd_h, z_inv_h, x_fwd_h, x_inv_h,
-    layer_out_h, field_grad_h, weight_grad_h,
-    field, cot, weight, y_fwd, y_inv, z_fwd, z_inv, x_fwd, x_inv, layer_out, field_grad, weight_grad,
+    gx, gy, zscales,
+    field_h, cot_h, weight_h, point, bias, y_fwd_h, z_fwd_h, z_inv_h, y_inv_h, x_fwd_h, x_inv_h,
+    layer_out_h, spec_h, grad_h, modes_h, local_h,
+    field, cot, weight, y_fwd, z_fwd, z_inv, y_inv, x_fwd, x_inv, layer_out,
     send_a, send_b, recv, grid_g, local, spec, grad, mode_grad, mix_a, mix_b, send_sem, recv_sem,
     load_sem, store_sem,
 ):
@@ -253,19 +254,26 @@
     chans, rows_x, rows_y, nz_len = field_h.shape
     half_rows = GC * rows_y
     halves = chans // GC
-    slab = recv.shape[2]
-    slab_half = slab // halves
-    lanes = recv.shape[3]
+    slab_half, lanes = recv.shape[3:]
     me_x, me_y = lax.axis_index("gx"), lax.axis_index("gy")
     me = me_x * gy + me_y
     half_modes = MZ * MX
 
     def peer(step):
-        other = lax.rem(me + step, peers)
+        down = peers - 1 - step
+        down = down - (down <= me).astype(jnp.int32)
+        up = step + (step >= me).astype(jnp.int32)
+        other = jnp.where(me < peers // 2, down, up)
         return other, {"gx": other // gy, "gy": lax.rem(other, gy)}
 
     barrier = pltpu.get_barrier_semaphore()
     loads = {}
+    stores = []
+
+    def store(source, target):
+        stores.append(pltpu.make_async_copy(source, target, store_sem.at[len(stores)]))
+        stores[-1].start()
+
 
     def load(name, *pairs):
         copies = []
@@ -299,50 +307,53 @@
         pl.semaphore_signal(barrier, inc=1, device_id=peer(step)[1], device_id_type=MESH)
         return carry
 
-    lax.fori_loop(1, peers, greet, 0)
-
-    def copy_to(phase, buffer, step):
+    lax.fori_loop(0, peers - 1, greet, 0, unroll=True)
+
+    def copy_to(phase, h, step):
         other, where = peer(step)
-        source = buffer.at[other] if buffer.shape[0] == peers else buffer.at[other // gy]
+        buffer = send_a.at[phase // 2, h, other] if phase % 2 == 0 else send_b.at[phase // 2, h, other // gy]
         return pltpu.make_async_remote_copy(
-            src_ref=source,
-            dst_ref=recv.at[phase, me],
-            send_sem=send_sem.at[phase, other],
-            recv_sem=recv_sem.at[phase, me],
+            src_ref=buffer,
+            dst_ref=recv.at[phase, h, me],
+            send_sem=send_sem.at[phase, h, other],
+            recv_sem=recv_sem.at[phase, h, me],
             device_id=where,
             device_id_type=MESH,
         )
 
-    def send(phase, buffer):
+    def send(phase, h):
         def one(step, carry):
-            copy_to(phase, buffer, step).start()
+            copy_to(phase, h, step).start()
             return carry
 
-        lax.fori_loop(1, peers, one, 0)
-        own = buffer[me] if buffer.shape[0] == peers else buffer[me_x]
-        recv[phase, me] = own
-
-    def receive(phase, buffer):
+        lax.fori_loop(0, peers - 1, one, 0, unroll=True)
+        if phase % 2 == 0:
+            recv[phase, h, me] = send_a[phase // 2, h, me]
+        else:
+            recv[phase, h, me] = send_b[phase // 2, h, me_x]
+
+    def receive(phase, h):
         def one(step, carry):
             other, where = peer(step)
             pltpu.make_async_remote_copy(
-                src_ref=recv.at[phase, other],
-                dst_ref=recv.at[phase, other],
-                send_sem=send_sem.at[phase, other],
-                recv_sem=recv_sem.at[phase, other],
+                src_ref=recv.at[phase, h, other],
+                dst_ref=recv.at[phase, h, other],
+                send_sem=send_sem.at[phase, h, other],
+                recv_sem=recv_sem.at[phase, h, other],
                 device_id=where,
                 device_id_type=MESH,
             ).wait_recv()
             return carry
 
-        lax.fori_loop(1, peers, one, 0)
-
-    def drain(phase, buffer):
+        lax.fori_loop(0, peers - 1, one, 0, unroll=True)
+
+    def drain(phase):
         def one(step, carry):
-            copy_to(phase, buffer, step).wait_send()
+            for h in range(halves):
+                copy_to(phase, h, step).wait_send()
             return carry
 
-        lax.fori_loop(1, peers, one, 0)
+        lax.fori_loop(0, peers - 1, one, 0, unroll=True)
 
     def zweight(width, scale_zero, scale_rest):
         lane = lax.broadcasted_iota(jnp.int32, (1, width), 1)
@@ -359,33 +370,28 @@
     def whole(grid):
         return grid[...].reshape(chans * rows_y, width)
 
-    def to_modes(grid, buffer, scale):
-        for h in range(halves):
-            after_y = dot(y_fwd[...], grid_half(grid, h))
-            rows = after_y.shape[0] // 2
-            both = jnp.concatenate([after_y[:rows], after_y[rows:]], axis=1).astype(BF)
-            out = (dot(both, z_fwd[...]) * scale).astype(BF)
-            buffer[:, h * slab_half : (h + 1) * slab_half, :] = out.reshape(peers, slab_half, lanes)
-
-    def owned(phase):
+    def to_modes(grid, phase, h, scale):
+        after_y = dot(y_fwd[...], grid_half(grid, h))
+        rows = after_y.shape[0] // 2
+        both = jnp.concatenate([after_y[:rows], after_y[rows:]], axis=1).astype(BF)
+        out = (dot(both, z_fwd[...]) * scale).astype(BF)
+        send_a[phase // 2, h] = out.reshape(peers, slab_half, lanes)
+
+    def owned(phase, h, store):
         parts = []
         for s in range(gx):
-            total = recv[phase, s * gy].astype(F32)
-            for t in range(1, gy):
-                total = total + recv[phase, s * gy + t].astype(F32)
+            total = recv[phase, h, s * gy].astype(F32)
+            for u in range(1, gy):
+                total = total + recv[phase, h, s * gy + u].astype(F32)
             parts.append(total)
-        return split_dot(jnp.concatenate(parts, axis=1), x_fwd[...])
-
-    def store_owned(values, store):
-        for h in range(halves):
-            for j in range(slab_half // GC):
-                rows = values[h * slab_half + j * GC : h * slab_half + (j + 1) * GC]
-                for r in range(2):
-                    store[r, h * GC : (h + 1) * GC, j * half_modes : (j + 1) * half_modes] = rows[
-                        :, r * half_modes : (r + 1) * half_modes
-                    ]
-
-    def to_slabs(store, buffer, scale):
+        values = split_dot(jnp.concatenate(parts, axis=1), x_fwd[...])
+        for j in range(slab_half // GC):
+            for r in range(2):
+                store[r, h * GC : (h + 1) * GC, j * half_modes : (j + 1) * half_modes] = values[
+                    j * GC : (j + 1) * GC, r * half_modes : (r + 1) * half_modes
+                ]
+
+    def to_slabs(store, phase, scale):
         rows = []
         for h in range(halves):
             for j in range(slab_half // GC):
@@ -401,14 +407,10 @@
         values = jnp.concatenate(rows, axis=0).astype(BF)
         out = (dot(values, x_inv[...]) * scale).astype(BF)
         for s in range(gx):
-            buffer[s] = out[:, s * lanes : (s + 1) * lanes]
-
-    def to_grid(phase, h):
-        modes = recv[phase, :, h * slab_half : (h + 1) * slab_half, :]
-        modes = modes.reshape(peers * slab_half, lanes)
-        after_z = dot(modes, z_inv[...]).astype(BF)
-        both = jnp.concatenate([after_z[:, :width], after_z[:, width:]], axis=0)
-        return dot(y_inv[...], both)
+            for h in range(halves):
+                send_b[phase // 2, h, s] = out[
+                    h * slab_half : (h + 1) * slab_half, s * lanes : (s + 1) * lanes
+                ]
 
     def spread(matrix):
         n = chans * rows_y
@@ -423,40 +425,46 @@
         return jnp.where(diag, wide, 0.0).astype(BF)
 
     loaded("field", "y_fwd", "z_fwd")
-    to_modes(field, send_a.at[0], fwd_scale)
-    pl.semaphore_wait(barrier, peers - 1)
-    send(0, send_a.at[0])
+    for h in range(halves):
+        to_modes(field, 0, h, fwd_scale)
+        if h == 0:
+            pl.semaphore_wait(barrier, peers - 1)
+        send(0, h)
     mix_a[...] = spread(point[...].T)
     mix_b[...] = spread(point[...])
     local[...] = dot(mix_a[...], whole(field))
-    receive(0, send_a.at[0])
-
-    loaded("x_fwd")
-    store_owned(owned(0), spec)
-    loaded("weight", "x_inv")
+
+    loaded("x_fwd", "weight", "x_inv")
     half = half_modes
+    mixed = {}
+    for h in range(halves):
+        receive(0, h)
+        owned(0, h, spec)
+        for j in range(slab_half // GC):
+            span = slice(j * half, (j + 1) * half)
+            mixed_r, mixed_i = mixed.get(j, (0.0, 0.0))
+            for c in range(h * GC, (h + 1) * GC):
+                w_r = weight[0, c, :, span].astype(F32)
+                w_i = weight[1, c, :, span].astype(F32)
+                s_r = spec[0, c : c + 1, span]
+                s_i = spec[1, c : c + 1, span]
+                mixed_r = mixed_r + (s_r * w_r - s_i * w_i)
+                mixed_i = mixed_i + (s_i * w_r + s_r * w_i)
+            mixed[j] = (mixed_r, mixed_i)
     for j in range(slab_half // GC):
         span = slice(j * half, (j + 1) * half)
-        mixed_r = jnp.zeros((chans, half), F32)
-        mixed_i = jnp.zeros((chans, half), F32)
-        for c in range(chans):
-            w_r = weight[0, c, :, span].astype(F32)
-            w_i = weight[1, c, :, span].astype(F32)
-            s_r = spec[0, c : c + 1, span]
-            s_i = spec[1, c : c + 1, span]
-            mixed_r = mixed_r + (s_r * w_r - s_i * w_i)
-            mixed_i = mixed_i + (s_i * w_r + s_r * w_i)
-        grad[0, :, span] = mixed_r
-        grad[1, :, span] = mixed_i
-    to_slabs(grad, send_b.at[0], zweight(gx * lanes, inv_zero, inv_rest))
-    send(1, send_b.at[0])
-    receive(1, send_b.at[0])
+        grad[0, :, span] = mixed[j][0]
+        grad[1, :, span] = mixed[j][1]
+    to_slabs(grad, 1, zweight(gx * lanes, inv_zero, inv_rest))
+    for h in range(halves):
+        send(1, h)
 
     loaded("z_inv", "y_inv", "cot")
     a = math.sqrt(2.0 / math.pi)
     for h in range(halves):
         rows = slice(h * half_rows, (h + 1) * half_rows)
-        pre_half = to_grid(1, h) + local[rows, :]
+        receive(1, h)
+        pre_half = to_grid(recv[1, h], z_inv[...], y_inv[...]) + local[rows, :]
         for c in range(GC):
             o = h * GC + c
             pre = pre_half[c * rows_y : (c + 1) * rows_y] + bias[o]
@@ -467,18 +475,17 @@
             slope = cdf + 0.5 * pre * (1.0 - t * t) * (a * (1.0 + 3.0 * 0.044715 * square))
             layer_out[o] = out
             grid_g[o] = (cot[o].astype(F32) * slope).astype(BF)
-    stores = [
-        pltpu.make_async_copy(s, d, store_sem.at[n])
-        for n, (d, s) in enumerate(by_x(layer_out_h, layer_out))
-    ]
-    for copy in stores:
-        copy.start()
-    to_modes(grid_g, send_a.at[1], zweight(lanes, inv_zero, inv_rest))
-    send(2, send_a.at[1])
+        some = slice(h * GC, (h + 1) * GC)
+        for target, source in by_x(layer_out_h.at[some], layer_out.at[some]):
+            store(source, target)
+        to_modes(grid_g, 2, h, zweight(lanes, inv_zero, inv_rest))
+        send(2, h)
     local[...] = dot(mix_b[...], whole(grid_g))
-    receive(2, send_a.at[1])
-
-    store_owned(owned(2), grad)
+    store(local, local_h)
+
+    for h in range(halves):
+        receive(2, h)
+        owned(2, h, grad)
     for j in range(slab_half // GC):
         span = slice(j * half, (j + 1) * half)
         g_r = grad[0, :, span]
@@ -488,32 +495,70 @@
             w_i = weight[1, c, :, span].astype(F32)
             mode_grad[0, c : c + 1, span] = jnp.sum(w_r * g_r + w_i * g_i, axis=0, keepdims=True)
             mode_grad[1, c : c + 1, span] = jnp.sum(w_r * g_i - w_i * g_r, axis=0, keepdims=True)
-    to_slabs(mode_grad, send_b.at[1], fwd_scale)
-    send(3, send_b.at[1])
-    for j in range(slab_half // GC):
-        span = slice(j * half, (j + 1) * half)
-        g_r = grad[0, :, span] * inv_wg
-        g_i = grad[1, :, span] * inv_wg
-        for c in range(chans):
-            s_r = spec[0, c : c + 1, span]
-            s_i = spec[1, c : c + 1, span]
-            weight_grad[0, c, :, span] = g_r * s_r + g_i * s_i
-            weight_grad[1, c, :, span] = g_i * s_r - g_r * s_i
-    stores.append(pltpu.make_async_copy(weight_grad, weight_grad_h, store_sem.at[len(stores)]))
-    stores[-1].start()
-    receive(3, send_b.at[1])
+    to_slabs(mode_grad, 3, fwd_scale)
     for h in range(halves):
-        total = to_grid(3, h) + local[h * half_rows : (h + 1) * half_rows, :]
-        field_grad[h * GC : (h + 1) * GC] = total.astype(BF).reshape(GC, rows_y, width)
-    for d, s in by_x(field_grad_h, field_grad):
-        stores.append(pltpu.make_async_copy(s, d, store_sem.at[len(stores)]))
-        stores[-1].start()
-    drain(0, send_a.at[0])
-    drain(1, send_b.at[0])
-    drain(2, send_a.at[1])
-    drain(3, send_b.at[1])
+        send(3, h)
+    store(spec, spec_h)
+    store(grad, grad_h)
+    for h in range(halves):
+        receive(3, h)
+        store(recv.at[3, h], modes_h.at[h])
+    for phase in range(4):
+        drain(phase)
     for copy in stores:
         copy.wait()
+
+
+def to_grid(modes, z_table, y_table):
+    peers, slab_half, lanes = modes.shape
+    after_z = dot(modes.reshape(peers * slab_half, lanes), z_table).astype(BF)
+    width = after_z.shape[1] // 2
+    both = jnp.concatenate([after_z[:, :width], after_z[:, width:]], axis=0)
+    return dot(y_table, both)
+
+
+def results(
+    wg_scale, first_h, spec_h, grad_h, modes_h, local_h, z_inv_h, y_inv_h,
+    layer_out_h, field_grad_h, weight_grad_h,
+    first, spec, grad, modes, local, z_inv, y_inv, field_grad, weight_grad, sem,
+):
+    chans, rows_x, rows_y, nz_len = layer_out_h.shape
+    half_rows = GC * rows_y
+
+    def copy(source, target):
+        copies.append(pltpu.make_async_copy(source, target, sem.at[len(copies)]))
+        copies[-1].start()
+
+    copies = []
+    copy(spec_h, spec)
+    copy(grad_h, grad)
+    copy(modes_h, modes)
+    copy(z_inv_h, z_inv)
+    copy(y_inv_h.at[lax.axis_index("gy")], y_inv)
+    copy(first_h, first)
+    copy(local_h, local)
+    copies[0].wait()
+    copies[1].wait()
+    quarter = chans // 4
+    for q in range(4):
+        some = slice(q * quarter, (q + 1) * quarter)
+        for c in range(q * quarter, (q + 1) * quarter):
+            s_r, s_i = spec[0, c : c + 1, :] * wg_scale, spec[1, c : c + 1, :] * wg_scale
+            weight_grad[0, c] = grad[0] * s_r + grad[1] * s_i
+            weight_grad[1, c] = grad[1] * s_r - grad[0] * s_i
+        copy(weight_grad.at[:, some], weight_grad_h.at[:, some])
+    copies[5].wait()
+    copy(first, layer_out_h)
+    for n in (2, 3, 4, 6):
+        copies[n].wait()
+    for h in range(modes.shape[0]):
+        some = slice(h * GC, (h + 1) * GC)
+        total = to_grid(modes[h], z_inv[...], y_inv[...]) + local[h * half_rows : (h + 1) * half_rows, :]
+        field_grad[some] = total.astype(BF).reshape(GC, rows_y, rows_x * nz_len)
+        for x in range(rows_x):
+            copy(field_grad.at[some, :, x * nz_len : (x + 1) * nz_len], field_grad_h.at[some, x])
+    for started in copies[7:]:
+        started.wait()
 
 
 def on_device_fused(gx, gy, field, cotangent, spectral_weight, point_weight, bias):
@@ -526,55 +571,84 @@
     zscales = (1.0 / math.sqrt(total_cells), inv, 2.0 * inv)
     wg_scale = math.sqrt(2.0 * mode_count / total_cells)
     tables = [jnp.asarray(t) for t in constant_tables(gx, gy, rows_x, rows_y, nz_len)]
-    slab = MY // peers * chans
+    y_fwd, y_inv, z_fwd, z_inv, x_fwd, x_inv = tables
+    halves = chans // GC
+    slab_half = MY // peers * GC
     lanes = 2 * MZ * rows_x
     rows, width = chans * rows_y, rows_x * nz_len
     vmem = pl.BlockSpec(memory_space=pltpu.VMEM)
+    smem = pl.BlockSpec(memory_space=pltpu.SMEM)
     hbm = pl.BlockSpec(memory_space=pltpu.HBM)
-    smem = pl.BlockSpec(memory_space=pltpu.SMEM)
-
     grid = pltpu.VMEM((chans, rows_y, width), BF)
-    held = [t.shape[1:] if n < 2 else t.shape for n, t in enumerate(tables)]
+    modes = pltpu.VMEM((2, chans, owned_modes), F32)
 
     def body(*refs):
-        fused(gx, gy, zscales, wg_scale, *refs)
-
+        fused(gx, gy, zscales, *refs)
+
+    layer_out, spec, grad, grad_modes, local = pl.pallas_call(
+        body,
+        out_shape=(
+            jax.ShapeDtypeStruct(field.shape, BF),
+            jax.ShapeDtypeStruct(modes.shape, F32),
+            jax.ShapeDtypeStruct(modes.shape, F32),
+            jax.ShapeDtypeStruct((halves, peers, slab_half, lanes), BF),
+            jax.ShapeDtypeStruct((rows, width), F32),
+        ),
+        in_specs=[hbm, hbm, hbm, vmem, smem] + [hbm] * 6,
+        out_specs=(hbm,) * 5,
+        scratch_shapes=[
+            grid,
+            grid,
+            pltpu.VMEM(spectral_weight.shape, BF),
+            pltpu.VMEM(y_fwd.shape[1:], BF),
+            pltpu.VMEM(z_fwd.shape, BF),
+            pltpu.VMEM(z_inv.shape, BF),
+            pltpu.VMEM(y_inv.shape[1:], BF),
+            pltpu.VMEM(x_fwd.shape, BF),
+            pltpu.VMEM(x_inv.shape, BF),
+            grid,
+            pltpu.VMEM((2, halves, peers, slab_half, lanes), BF),
+            pltpu.VMEM((2, halves, gx, slab_half, lanes), BF),
+            pltpu.VMEM((4, halves, peers, slab_half, lanes), BF),
+            grid,
+            pltpu.VMEM((rows, width), F32),
+            modes,
+            modes,
+            modes,
+            pltpu.VMEM((rows, rows), BF),
+            pltpu.VMEM((rows, rows), BF),
+            pltpu.SemaphoreType.DMA((4, halves, peers)),
+            pltpu.SemaphoreType.DMA((4, halves, peers)),
+            pltpu.SemaphoreType.DMA((2 * rows_x + 7,)),
+            pltpu.SemaphoreType.DMA((halves * (rows_x + 1) + 3,)),
+        ],
+        compiler_params=pltpu.CompilerParams(
+            collective_id=0, has_side_effects=True, vmem_limit_bytes=56 * 1024 * 1024
+        ),
+    )(field, cotangent, spectral_weight, point_weight, bias, y_fwd, z_fwd, z_inv, y_inv, x_fwd, x_inv)
     return pl.pallas_call(
-        body,
+        functools.partial(results, wg_scale),
         out_shape=(
             jax.ShapeDtypeStruct(field.shape, BF),
             jax.ShapeDtypeStruct(field.shape, BF),
             jax.ShapeDtypeStruct(spectral_weight.shape, F32),
         ),
-        in_specs=[hbm, hbm, hbm, vmem, smem] + [hbm] * 6,
+        in_specs=[hbm] * 7,
         out_specs=(hbm, hbm, hbm),
         scratch_shapes=[
-            grid,
-            grid,
-            pltpu.VMEM(spectral_weight.shape, BF),
-            *[pltpu.VMEM(s, BF) for s in held],
-            grid,
+            pltpu.VMEM(field.shape, BF),
+            modes,
+            modes,
+            pltpu.VMEM(grad_modes.shape, BF),
+            pltpu.VMEM(local.shape, F32),
+            pltpu.VMEM(z_inv.shape, BF),
+            pltpu.VMEM(y_inv.shape[1:], BF),
             grid,
             pltpu.VMEM(spectral_weight.shape, F32),
-            pltpu.VMEM((2, peers, slab, lanes), BF),
-            pltpu.VMEM((2, gx, slab, lanes), BF),
-            pltpu.VMEM((4, peers, slab, lanes), BF),
-            grid,
-            pltpu.VMEM((rows, width), F32),
-            pltpu.VMEM((2, chans, owned_modes), F32),
-            pltpu.VMEM((2, chans, owned_modes), F32),
-            pltpu.VMEM((2, chans, owned_modes), F32),
-            pltpu.VMEM((rows, rows), BF),
-            pltpu.VMEM((rows, rows), BF),
-            pltpu.SemaphoreType.DMA((4, peers)),
-            pltpu.SemaphoreType.DMA((4, peers)),
-            pltpu.SemaphoreType.DMA((2 * rows_x + 7,)),
-            pltpu.SemaphoreType.DMA((2 * rows_x + 1,)),
+            pltpu.SemaphoreType.DMA((12 + halves * rows_x,)),
         ],
-        compiler_params=pltpu.CompilerParams(
-            collective_id=0, has_side_effects=True, vmem_limit_bytes=56 * 1024 * 1024
-        ),
-    )(field, cotangent, spectral_weight, point_weight, bias, *tables)
+        compiler_params=pltpu.CompilerParams(vmem_limit_bytes=56 * 1024 * 1024),
+    )(layer_out, spec, grad, grad_modes, local, z_inv, y_inv)
 
 
 def solution(mesh):

time: 40.3 us -> 37.6 us (0.933)
  local copies, waits for them, and re-layouts: 5.23 us -> 0 us
  Pallas kernels: 34.2 us -> 36.8 us
    unnamed x5 -> x0, local copies, waits for them, and re-layouts: 5.23 us -> none
    pallas_call x0 -> x1, Pallas kernels: none -> 3.62 us  [on_device_fused(): pl.pallas_call(functools.partial(results, wg_scale), out_shape=(jax.Shape...]
    pallas_call x1, Pallas kernels: 34.2 us -> 33.1 us  [on_device_fused(): pl.pallas_call(body, out_shape=(jax.ShapeDtypeStruct(field.shape, BF), ja...]
where the time goes in v3:
time: 37.6 us; the launch traced here: 37.4 us
  Pallas kernels  36.8 us (98%)
  between operations  0.64 us (2%)
    pallas_call x1, Pallas kernels, on_device_fused(): pl.pallas_call(body, out_shape=(jax.ShapeDtypeStruct(field.shape, BF), ja...  33.1 us
    pallas_call x1, Pallas kernels, on_device_fused(): pl.pallas_call(functools.partial(results, wg_scale), out_shape=(jax.Shape...  3.62 us

profile of v3, /device:TPU:0, one launch (start us, length us, event | category | flops | bytes accessed | tf_op | source)
XLA Modules:
  0.0 37.4 jit_solution(3281742786488658231)
XLA Ops:
  0.6 33.1 %shard_map.130 = (bf16[16,4,32,128]{3,2,1,0:T(8,128)(2,1)}, f32[2,16,1024]{2,1,0:T(8,128)}, f32[2,16,1024]{2,1,0:T(8,128)}, bf16[2,16,16,128]{3,2,1,0:T(8,128)(2,1)}, f32[512,512]{1,0:T(8,128)}) custom-call(bf16[16,4,32,128]{3,2,1,0:T(8,128)(2,1)} %refs_0_.1, bf16[16,4,32,128]{3,2,1,0:T(8,128)(2,1)} %refs_1_.1, bf16[2,16,16,1024]{3,2,1,0:T(8,128)(2,1)} %refs_2_.1, ...), custom_call_target="tpu_custom_call" | custom-call | tf_op jit(solution)/shard_map/pallas_call | solution.py:588
  33.8 3.6 %shard_map.131 = (bf16[16,4,32,128]{3,2,1,0:T(8,128)(2,1)}, bf16[16,4,32,128]{3,2,1,0:T(8,128)(2,1)}, f32[2,16,16,1024]{3,2,1,0:T(8,128)}) custom-call(bf16[16,4,32,128]{3,2,1,0:T(8,128)(2,1)} %get-tuple-element.8.first_h, f32[2,16,1024]{2,1,0:T(8,128)} %get-tuple-element.9.spec_h, f32[2,16,1024]{2,1,0:T(8,128)} %get-tuple-element.10.grad_h, ...), custom_call_target="tpu_custom_call" | custom-call | tf_op jit(solution)/shard_map/pallas_call | solution.py:629

commit v4 on v3

--- a/solution.py
+++ b/solution.py
@@ -244,9 +244,9 @@
 
 def fused(
     gx, gy, zscales,
-    field_h, cot_h, weight_h, point, bias, y_fwd_h, z_fwd_h, z_inv_h, y_inv_h, x_fwd_h, x_inv_h,
+    field_h, cot_h, weight_h, point_h, bias_h, y_fwd_h, z_fwd_h, z_inv_h, y_inv_h, x_fwd_h, x_inv_h,
     layer_out_h, spec_h, grad_h, modes_h, local_h,
-    field, cot, weight, y_fwd, z_fwd, z_inv, y_inv, x_fwd, x_inv, layer_out,
+    field, cot, weight, point, bias, y_fwd, z_fwd, z_inv, y_inv, x_fwd, x_inv, layer_out,
     send_a, send_b, recv, grid_g, local, spec, grad, mode_grad, mix_a, mix_b, send_sem, recv_sem,
     load_sem, store_sem,
 ):
@@ -296,6 +296,8 @@
     load("field", *by_x(field_h, field))
     load("y_fwd", (y_fwd_h.at[me_y], y_fwd))
     load("z_fwd", (z_fwd_h, z_fwd))
+    load("point", (point_h, point))
+    load("bias", (bias_h, bias))
     load("x_fwd", (x_fwd_h, x_fwd))
     load("weight", (weight_h, weight))
     load("x_inv", (x_inv_h, x_inv))
@@ -315,8 +317,8 @@
         return pltpu.make_async_remote_copy(
             src_ref=buffer,
             dst_ref=recv.at[phase, h, me],
-            send_sem=send_sem.at[phase, h, other],
-            recv_sem=recv_sem.at[phase, h, me],
+            send_sem=send_sem.at[phase, h],
+            recv_sem=recv_sem.at[phase, h],
             device_id=where,
             device_id_type=MESH,
         )
@@ -332,28 +334,23 @@
         else:
             recv[phase, h, me] = send_b[phase // 2, h, me_x]
 
+    def all_slabs(phase, h):
+        slabs = recv.at[phase, h, pl.ds(0, peers - 1)]
+        return pltpu.make_async_remote_copy(
+            src_ref=slabs,
+            dst_ref=slabs,
+            send_sem=send_sem.at[phase, h],
+            recv_sem=recv_sem.at[phase, h],
+            device_id=peer(0)[1],
+            device_id_type=MESH,
+        )
+
     def receive(phase, h):
-        def one(step, carry):
-            other, where = peer(step)
-            pltpu.make_async_remote_copy(
-                src_ref=recv.at[phase, h, other],
-                dst_ref=recv.at[phase, h, other],
-                send_sem=send_sem.at[phase, h, other],
-                recv_sem=recv_sem.at[phase, h, other],
-                device_id=where,
-                device_id_type=MESH,
-            ).wait_recv()
-            return carry
-
-        lax.fori_loop(0, peers - 1, one, 0, unroll=True)
+        all_slabs(phase, h).wait_recv()
 
     def drain(phase):
-        def one(step, carry):
-            for h in range(halves):
-                copy_to(phase, h, step).wait_send()
-            return carry
-
-        lax.fori_loop(0, peers - 1, one, 0, unroll=True)
+        for h in range(halves):
+            all_slabs(phase, h).wait_send()
 
     def zweight(width, scale_zero, scale_rest):
         lane = lax.broadcasted_iota(jnp.int32, (1, width), 1)
@@ -427,9 +424,10 @@
     loaded("field", "y_fwd", "z_fwd")
     for h in range(halves):
         to_modes(field, 0, h, fwd_scale)
-        if h == 0:
-            pl.semaphore_wait(barrier, peers - 1)
+    pl.semaphore_wait(barrier, peers - 1)
+    for h in range(halves):
         send(0, h)
+    loaded("point", "bias")
     mix_a[...] = spread(point[...].T)
     mix_b[...] = spread(point[...])
     local[...] = dot(mix_a[...], whole(field))
@@ -458,6 +456,7 @@
     to_slabs(grad, 1, zweight(gx * lanes, inv_zero, inv_rest))
     for h in range(halves):
         send(1, h)
+    drain(0)
 
     loaded("z_inv", "y_inv", "cot")
     a = math.sqrt(2.0 / math.pi)
@@ -480,6 +479,7 @@
             store(source, target)
         to_modes(grid_g, 2, h, zweight(lanes, inv_zero, inv_rest))
         send(2, h)
+    drain(1)
     local[...] = dot(mix_b[...], whole(grid_g))
     store(local, local_h)
 
@@ -498,13 +498,13 @@
     to_slabs(mode_grad, 3, fwd_scale)
     for h in range(halves):
         send(3, h)
+    drain(2)
     store(spec, spec_h)
     store(grad, grad_h)
     for h in range(halves):
         receive(3, h)
         store(recv.at[3, h], modes_h.at[h])
-    for phase in range(4):
-        drain(phase)
+    drain(3)
     for copy in stores:
         copy.wait()
 
@@ -576,8 +576,6 @@
     slab_half = MY // peers * GC
     lanes = 2 * MZ * rows_x
     rows, width = chans * rows_y, rows_x * nz_len
-    vmem = pl.BlockSpec(memory_space=pltpu.VMEM)
-    smem = pl.BlockSpec(memory_space=pltpu.SMEM)
     hbm = pl.BlockSpec(memory_space=pltpu.HBM)
     grid = pltpu.VMEM((chans, rows_y, width), BF)
     modes = pltpu.VMEM((2, chans, owned_modes), F32)
@@ -594,12 +592,14 @@
             jax.ShapeDtypeStruct((halves, peers, slab_half, lanes), BF),
             jax.ShapeDtypeStruct((rows, width), F32),
         ),
-        in_specs=[hbm, hbm, hbm, vmem, smem] + [hbm] * 6,
+        in_specs=[hbm] * 11,
         out_specs=(hbm,) * 5,
         scratch_shapes=[
             grid,
             grid,
             pltpu.VMEM(spectral_weight.shape, BF),
+            pltpu.VMEM(point_weight.shape, BF),
+            pltpu.SMEM(bias.shape, F32),
             pltpu.VMEM(y_fwd.shape[1:], BF),
             pltpu.VMEM(z_fwd.shape, BF),
             pltpu.VMEM(z_inv.shape, BF),
@@ -617,9 +617,9 @@
             modes,
             pltpu.VMEM((rows, rows), BF),
             pltpu.VMEM((rows, rows), BF),
-            pltpu.SemaphoreType.DMA((4, halves, peers)),
-            pltpu.SemaphoreType.DMA((4, halves, peers)),
-            pltpu.SemaphoreType.DMA((2 * rows_x + 7,)),
+            pltpu.SemaphoreType.DMA((4, halves)),
+            pltpu.SemaphoreType.DMA((4, halves)),
+            pltpu.SemaphoreType.DMA((2 * rows_x + 9,)),
             pltpu.SemaphoreType.DMA((halves * (rows_x + 1) + 3,)),
         ],
         compiler_params=pltpu.CompilerParams(

time: 37.6 us -> 34.5 us (0.918)
  Pallas kernels: 36.8 us -> 33.7 us
    pallas_call x1, Pallas kernels: 33.1 us -> 30.1 us  [on_device_fused(): pl.pallas_call(body, out_shape=(jax.ShapeDtypeStruct(field.shape, BF), ja...]
where the time goes in v4:
time: 34.5 us; the launch traced here: 34.3 us
  Pallas kernels  33.7 us (98%)
  between operations  0.64 us (2%)
    pallas_call x1, Pallas kernels, on_device_fused(): pl.pallas_call(body, out_shape=(jax.ShapeDtypeStruct(field.shape, BF), ja...  30.1 us
    pallas_call x1, Pallas kernels, on_device_fused(): pl.pallas_call(functools.partial(results, wg_scale), out_shape=(jax.Shape...  3.61 us

profile of v4, /device:TPU:0, one launch (start us, length us, event | category | flops | bytes accessed | tf_op | source)
XLA Modules:
  0.0 34.3 jit_solution(12799263249639761072)
XLA Ops:
  0.6 30.1 %shard_map.130 = (bf16[16,4,32,128]{3,2,1,0:T(8,128)(2,1)}, f32[2,16,1024]{2,1,0:T(8,128)}, f32[2,16,1024]{2,1,0:T(8,128)}, bf16[2,16,16,128]{3,2,1,0:T(8,128)(2,1)}, f32[512,512]{1,0:T(8,128)}) custom-call(bf16[16,4,32,128]{3,2,1,0:T(8,128)(2,1)} %refs_0_.1, bf16[16,4,32,128]{3,2,1,0:T(8,128)(2,1)} %refs_1_.1, bf16[2,16,16,1024]{3,2,1,0:T(8,128)(2,1)} %refs_2_.1, ...), custom_call_target="tpu_custom_call" | custom-call | tf_op jit(solution)/shard_map/pallas_call | solution.py:586
  30.7 3.6 %shard_map.131 = (bf16[16,4,32,128]{3,2,1,0:T(8,128)(2,1)}, bf16[16,4,32,128]{3,2,1,0:T(8,128)(2,1)}, f32[2,16,16,1024]{3,2,1,0:T(8,128)}) custom-call(bf16[16,4,32,128]{3,2,1,0:T(8,128)(2,1)} %get-tuple-element.8.first_h, f32[2,16,1024]{2,1,0:T(8,128)} %get-tuple-element.9.spec_h, f32[2,16,1024]{2,1,0:T(8,128)} %get-tuple-element.10.grad_h, ...), custom_call_target="tpu_custom_call" | custom-call | tf_op jit(solution)/shard_map/pallas_call | solution.py:629

commit v5 on v4

--- a/solution.py
+++ b/solution.py
@@ -351,6 +351,17 @@
     def drain(phase):
         for h in range(halves):
             all_slabs(phase, h).wait_send()
+
+    def last_copy(step):
+        other, where = peer(step)
+        return pltpu.make_async_remote_copy(
+            src_ref=send_b.at[1, :, other // gy],
+            dst_ref=recv.at[3, :, me],
+            send_sem=send_sem.at[3, 0],
+            recv_sem=recv_sem.at[3, 0],
+            device_id=where,
+            device_id_type=MESH,
+        )
 
     def zweight(width, scale_zero, scale_rest):
         lane = lax.broadcasted_iota(jnp.int32, (1, width), 1)
@@ -496,15 +507,24 @@
             mode_grad[0, c : c + 1, span] = jnp.sum(w_r * g_r + w_i * g_i, axis=0, keepdims=True)
             mode_grad[1, c : c + 1, span] = jnp.sum(w_r * g_i - w_i * g_r, axis=0, keepdims=True)
     to_slabs(mode_grad, 3, fwd_scale)
-    for h in range(halves):
-        send(3, h)
+    for step in range(peers - 1):
+        last_copy(step).start()
+    recv[3, :, me] = send_b[1, :, me_x]
     drain(2)
     store(spec, spec_h)
     store(grad, grad_h)
-    for h in range(halves):
-        receive(3, h)
-        store(recv.at[3, h], modes_h.at[h])
-    drain(3)
+    slabs = recv.at[3, :, pl.ds(0, peers - 1)]
+    whole_copy = pltpu.make_async_remote_copy(
+        src_ref=slabs,
+        dst_ref=slabs,
+        send_sem=send_sem.at[3, 0],
+        recv_sem=recv_sem.at[3, 0],
+        device_id=peer(0)[1],
+        device_id_type=MESH,
+    )
+    whole_copy.wait_recv()
+    store(recv.at[3], modes_h)
+    whole_copy.wait_send()
     for copy in stores:
         copy.wait()
 

time: 34.5 us -> 33.7 us (0.977)
  Pallas kernels: 33.7 us -> 32.9 us
    pallas_call x1, Pallas kernels: 30.1 us -> 29.2 us  [on_device_fused(): pl.pallas_call(body, out_shape=(jax.ShapeDtypeStruct(field.shape, BF), ja...]
where the time goes in v5:
time: 33.7 us; the launch traced here: 33.5 us
  Pallas kernels  32.9 us (98%)
  between operations  0.64 us (2%)
    pallas_call x1, Pallas kernels, on_device_fused(): pl.pallas_call(body, out_shape=(jax.ShapeDtypeStruct(field.shape, BF), ja...  29.2 us
    pallas_call x1, Pallas kernels, on_device_fused(): pl.pallas_call(functools.partial(results, wg_scale), out_shape=(jax.Shape...  3.61 us

profile of v5, /device:TPU:0, one launch (start us, length us, event | category | flops | bytes accessed | tf_op | source)
XLA Modules:
  0.0 33.5 jit_solution(2106030979832469997)
XLA Ops:
  0.6 29.2 %shard_map.130 = (bf16[16,4,32,128]{3,2,1,0:T(8,128)(2,1)}, f32[2,16,1024]{2,1,0:T(8,128)}, f32[2,16,1024]{2,1,0:T(8,128)}, bf16[2,16,16,128]{3,2,1,0:T(8,128)(2,1)}, f32[512,512]{1,0:T(8,128)}) custom-call(bf16[16,4,32,128]{3,2,1,0:T(8,128)(2,1)} %refs_0_.1, bf16[16,4,32,128]{3,2,1,0:T(8,128)(2,1)} %refs_1_.1, bf16[2,16,16,1024]{3,2,1,0:T(8,128)(2,1)} %refs_2_.1, ...), custom_call_target="tpu_custom_call" | custom-call | tf_op jit(solution)/shard_map/pallas_call | solution.py:606
  29.9 3.6 %shard_map.131 = (bf16[16,4,32,128]{3,2,1,0:T(8,128)(2,1)}, bf16[16,4,32,128]{3,2,1,0:T(8,128)(2,1)}, f32[2,16,16,1024]{3,2,1,0:T(8,128)}) custom-call(bf16[16,4,32,128]{3,2,1,0:T(8,128)(2,1)} %get-tuple-element.8.first_h, f32[2,16,1024]{2,1,0:T(8,128)} %get-tuple-element.9.spec_h, f32[2,16,1024]{2,1,0:T(8,128)} %get-tuple-element.10.grad_h, ...), custom_call_target="tpu_custom_call" | custom-call | tf_op jit(solution)/shard_map/pallas_call | solution.py:649
